TPU v7x, 32 devices: a whole 2x2x4 slice. The times are simulated.
32 devices in a mesh: fsdp: 8 (over z, core), mp: 4 (over y, x).
Axes of the slice: x: 2, y: 2, z: 4, core: 2. Of those that a mesh axis runs over, the one named last changes fastest.
Arguments:
- inputs: bfloat16 [2048, 2048], P('fsdp'), may hold values from -6 to 6
- cotangent: bfloat16 [2048, 2048], P('fsdp'), may hold values from -6 to 6
- lengths: int32 [2], replicated, may hold values from 256 to 1024, as said below
- attn_scale: float32 [2048], P('fsdp'), may hold values from 0.5 to 1.5
- w_query: float32 [2048, 2048], P('fsdp', 'mp'), may hold values from -0.015625 to 0.015625
- w_key: float32 [2048, 2048], P('fsdp', 'mp'), may hold values from -0.125 to 0.125
- w_value: float32 [2048, 2048], P('fsdp', 'mp'), may hold values from -0.125 to 0.125
- w_out: float32 [2048, 2048], P('mp', 'fsdp'), may hold values from -3 to 3
- rel_table: float32 [32, 32], P('fsdp', 'mp'), may hold values from -4 to 4
- ffn_scale: float32 [2048], P('fsdp'), may hold values from 0.5 to 1.5
- w_gate: float32 [2048, 5120], P('fsdp', 'mp'), may hold values from -0.125 to 0.125
- w_up: float32 [2048, 5120], P('fsdp', 'mp'), may hold values from -0.125 to 0.125
- w_down: float32 [5120, 2048], P('mp', 'fsdp'), may hold values from -0.078125 to 0.078125
Outputs:
- outputs: bfloat16 [2048, 2048], P('fsdp')
- d_inputs: bfloat16 [2048, 2048], P('fsdp')
- d_attn_scale: float32 [2048], P('fsdp')
- d_w_query: float32 [2048, 2048], P('fsdp', 'mp')
- d_w_key: float32 [2048, 2048], P('fsdp', 'mp')
- d_w_value: float32 [2048, 2048], P('fsdp', 'mp')
- d_w_out: float32 [2048, 2048], P('mp', 'fsdp')
- d_rel_table: float32 [32, 32], P('fsdp', 'mp')
- d_ffn_scale: float32 [2048], P('fsdp')
- d_w_gate: float32 [2048, 5120], P('fsdp', 'mp')
- d_w_up: float32 [2048, 5120], P('fsdp', 'mp')
- d_w_down: float32 [5120, 2048], P('mp', 'fsdp')
Inputs may be any that keep to these rules, and one draw needn't show every extreme that they name: lengths[s] slots at the start of sequence s are used, the rest is padding; in every draw some sequence is full.
All inputs are finite; a program needn't handle non-finite values.
Results may differ from a plain program's by a relative error of at most 0.019.
Values may be sent and summed in bfloat16 or wider, within the bound.
No kernel may reach another device: no remote copies, remote signals or barrier semaphores. Data moves between devices by JAX's collectives and lax.ppermute only.
A program may use at most 192 MiB of HBM per device.

v0:
```python
import functools

import jax
import jax.numpy as jnp
from jax import lax
from jax.experimental import pallas as pl
from jax.experimental.pallas import tpu as pltpu
from jax.sharding import Mesh, PartitionSpec as P

LOW = jnp.bfloat16
F32 = jnp.float32
CORES = 2
THRESHOLDS = (12, 16, 23, 32, 46, 64, 91)
EPSILON = 1e-06
MASKED = -1e30
SKEW = 128


def bucket_of(rel_offset):
    distance = jnp.abs(rel_offset)
    far_bucket = 8 + sum(((distance >= threshold).astype(jnp.int32) for threshold in THRESHOLDS))
    bucket_abs = jnp.where(distance < 8, distance, far_bucket)
    return bucket_abs + jnp.where(rel_offset > 0, 16, 0)


def bucket_onehot(buckets, seq_len):
    offset = lax.broadcasted_iota(jnp.int32, (buckets, 2 * seq_len), 1) - seq_len
    bucket = lax.broadcasted_iota(jnp.int32, (buckets, 2 * seq_len), 0)
    return bucket_of(offset) == bucket


def head_lanes(rows, width, head_width, head):
    lane = lax.broadcasted_iota(jnp.int32, (rows, width), 1)
    return (lane >= head * head_width) & (lane < (head + 1) * head_width)


def only(mask, values):
    return jnp.where(mask, values, jnp.zeros_like(values))


def block_place(block, core, near_count):
    return lax.rem(block, near_count) * CORES + lax.bitwise_xor(lax.div(block, near_count), core)


def bias_places(place_ref, step, blocks, rows, seq_len):
    core, near_count = place_ref[1], blocks // CORES
    query = block_place(step, core, near_count) * rows
    return [
        [
            pl.multiple_of(
                block_place(block, core, near_count) * rows - query - part * SKEW + seq_len - SKEW,
                SKEW,
            )
            for block in range(blocks)
        ]
        for part in range(rows // SKEW)
    ]


def forward_kernel(heads, rows, place_ref, qkv_ref, table_ref, o_ref, p_ref, skew_ref):
    step = pl.program_id(0)
    seq_len = qkv_ref.shape[0]
    width = qkv_ref.shape[1] // 3
    head_width = width // heads
    span = 2 * seq_len
    blocks = seq_len // rows

    @pl.when(step == 0)
    def _():
        one_hot = bucket_onehot(table_ref.shape[1], seq_len).astype(F32).astype(LOW)
        lines = jnp.dot(table_ref[...], one_hot, preferred_element_type=F32)
        for head in range(heads):
            line = jnp.broadcast_to(lines[head : head + 1], (SKEW, span))
            skew_ref[head] = pltpu.roll(line, span - SKEW, 1, stride=1, stride_axis=0)

    row = lax.broadcasted_iota(jnp.int32, (1, rows), 1)
    allowed = jnp.concatenate(
        [
            block_place(block, place_ref[1], blocks // CORES) * rows + row < place_ref[0]
            for block in range(blocks)
        ],
        1,
    )
    queries = qkv_ref[pl.ds(pl.multiple_of(step * rows, rows), rows), :width]
    keys = qkv_ref[:, width : 2 * width]
    values = qkv_ref[:, 2 * width :]
    total = jnp.zeros((rows, width), F32)
    places = bias_places(place_ref, step, blocks, rows, seq_len)
    for head in range(heads):
        scores = lax.dot_general(
            only(head_lanes(rows, width, head_width, head), queries),
            keys,
            (((1,), (1,)), ((), ())),
            preferred_element_type=F32,
        )
        bias = jnp.concatenate(
            [
                jnp.concatenate([skew_ref[head, :, pl.ds(place, rows)] for place in part], 1)
                for part in places
            ],
            0,
        )
        scores = jnp.where(allowed, scores + bias, MASKED)
        grown = jnp.exp(scores - jnp.max(scores, axis=1, keepdims=True))
        prob = (grown * (1.0 / jnp.sum(grown, axis=1, keepdims=True))).astype(LOW)
        p_ref[head] = prob
        total = total + jnp.dot(
            prob,
            only(head_lanes(seq_len, width, head_width, head), values),
            preferred_element_type=F32,
        )
    o_ref[...] = total.astype(LOW)


def attention_forward(qkv, table, place, heads, rows):
    seq_len, width = qkv.shape[0], qkv.shape[1] // 3
    return pl.pallas_call(
        functools.partial(forward_kernel, heads, rows),
        grid=(seq_len // rows,),
        in_specs=[
            pl.BlockSpec(memory_space=pltpu.SMEM),
            pl.BlockSpec(qkv.shape, lambda i: (0, 0)),
            pl.BlockSpec(table.shape, lambda i: (0, 0)),
        ],
        out_specs=[
            pl.BlockSpec((rows, width), lambda i: (i, 0)),
            pl.BlockSpec((heads, rows, seq_len), lambda i: (0, i, 0)),
        ],
        out_shape=[
            jax.ShapeDtypeStruct((seq_len, width), LOW),
            jax.ShapeDtypeStruct((heads, seq_len, seq_len), LOW),
        ],
        scratch_shapes=[pltpu.VMEM((heads, SKEW, 2 * seq_len), F32)],
        compiler_params=pltpu.CompilerParams(vmem_limit_bytes=32 * 2**20),
        cost_estimate=pl.CostEstimate(
            flops=4 * seq_len * seq_len * width,
            bytes_accessed=2 * heads * seq_len * seq_len,
            transcendentals=0,
        ),
        name="attention_forward",
    )(place, qkv, table)


def backward_kernel(
    heads, rows, place_ref, p_ref, do_ref, qkv_ref, d_ref, dt_ref, dk_sum, dv_sum, skew_ref
):
    step = pl.program_id(0)
    seq_len = qkv_ref.shape[0]
    width = qkv_ref.shape[1] // 3
    head_width = width // heads
    span = 2 * seq_len
    blocks = seq_len // rows

    @pl.when(step == 0)
    def _():
        dk_sum[...] = jnp.zeros_like(dk_sum)
        dv_sum[...] = jnp.zeros_like(dv_sum)
        skew_ref[...] = jnp.zeros_like(skew_ref)

    here = pl.ds(pl.multiple_of(step * rows, rows), rows)
    queries = qkv_ref[here, :width]
    keys = qkv_ref[:, width : 2 * width]
    values = qkv_ref[:, 2 * width :]
    grads = do_ref[...]
    total = jnp.zeros((rows, width), F32)
    places = bias_places(place_ref, step, blocks, rows, seq_len)
    for head in range(heads):
        own = head_lanes(rows, width, head_width, head)
        own_grads = only(own, grads)
        d_prob = lax.dot_general(
            own_grads, values, (((1,), (1,)), ((), ())), preferred_element_type=F32
        )
        prob_low = p_ref[head]
        prob = prob_low.astype(F32)
        weighed = prob * d_prob
        d_scores = (weighed - prob * jnp.sum(weighed, axis=1, keepdims=True)).astype(LOW)
        total = total + jnp.dot(
            d_scores,
            only(head_lanes(seq_len, width, head_width, head), keys),
            preferred_element_type=F32,
        )
        dk_sum[...] += lax.dot_general(
            d_scores, only(own, queries), (((0,), (0,)), ((), ())), preferred_element_type=F32
        )
        dv_sum[...] += lax.dot_general(
            prob_low, own_grads, (((0,), (0,)), ((), ())), preferred_element_type=F32
        )
        for part in range(rows // SKEW):
            for block in range(blocks):
                skew_ref[head, :, pl.ds(places[part][block], rows)] += d_scores[
                    part * SKEW : (part + 1) * SKEW, block * rows : (block + 1) * rows
                ].astype(F32)
    d_ref[here, :width] = total.astype(LOW)

    @pl.when(step == pl.num_programs(0) - 1)
    def _():
        d_ref[:, width : 2 * width] = dk_sum[...].astype(LOW)
        d_ref[:, 2 * width :] = dv_sum[...].astype(LOW)
        one_hot = bucket_onehot(dt_ref.shape[0], seq_len)
        row = lax.broadcasted_iota(jnp.int32, (SKEW, span), 0)
        column = lax.broadcasted_iota(jnp.int32, dt_ref.shape, 1)
        result = jnp.zeros(dt_ref.shape, F32)
        for head in range(heads):
            level = pltpu.roll(skew_ref[head], SKEW, 1)
            bit = 1
            while bit < SKEW:
                level = jnp.where((row & bit) != 0, pltpu.roll(level, span - bit, 1), level)
                bit *= 2
            line = jnp.sum(level, axis=0, keepdims=True)
            summed = jnp.sum(jnp.where(one_hot, line, 0.0), axis=1, keepdims=True)
            result = jnp.where(column == head, summed, result)
        dt_ref[...] = result


def attention_backward(prob, d_out, qkv, place, heads, rows, buckets):
    seq_len, width = d_out.shape
    return pl.pallas_call(
        functools.partial(backward_kernel, heads, rows),
        grid=(seq_len // rows,),
        in_specs=[
            pl.BlockSpec(memory_space=pltpu.SMEM),
            pl.BlockSpec((heads, rows, seq_len), lambda i: (0, i, 0)),
            pl.BlockSpec((rows, width), lambda i: (i, 0)),
            pl.BlockSpec(qkv.shape, lambda i: (0, 0)),
        ],
        out_specs=[
            pl.BlockSpec(qkv.shape, lambda i: (0, 0)),
            pl.BlockSpec((buckets, 128), lambda i: (0, 0)),
        ],
        out_shape=[
            jax.ShapeDtypeStruct(qkv.shape, LOW),
            jax.ShapeDtypeStruct((buckets, 128), F32),
        ],
        scratch_shapes=[
            pltpu.VMEM((seq_len, width), F32),
            pltpu.VMEM((seq_len, width), F32),
            pltpu.VMEM((heads, SKEW, 2 * seq_len), F32),
        ],
        compiler_params=pltpu.CompilerParams(vmem_limit_bytes=40 * 2**20),
        cost_estimate=pl.CostEstimate(
            flops=8 * seq_len * seq_len * width * 4,
            bytes_accessed=2 * heads * seq_len * seq_len,
            transcendentals=0,
        ),
        name="attention_backward",
    )(place, prob, d_out, qkv)


COLUMN = ("seq", "near", "core")
EXTRA = 8


def exchange(blocks, axes):
    return lax.all_to_all(blocks, axes, split_axis=0, concat_axis=0, tiled=True)


def swap(block, axis):
    return lax.ppermute(block, axis, [(0, 1), (1, 0)])


def after(value, *done):
    return lax.optimization_barrier((value,) + done)[0]


def rows_dot(left, right):
    return jnp.dot(left, right, preferred_element_type=F32)


def contract_cols(left, right):
    return lax.dot_general(left, right, (((1,), (1,)), ((), ())), preferred_element_type=F32)


def contract_rows(left, right):
    return lax.dot_general(left, right, (((0,), (0,)), ((), ())), preferred_element_type=F32)


def rms(values):
    return lax.rsqrt(jnp.mean(values * values, axis=-1, keepdims=True) + EPSILON)


def norm_grad(inner, normed, inverse):
    return inverse * (inner - normed * jnp.mean(inner * normed, axis=-1, keepdims=True))


def gelu_tanh(values):
    return jax.nn.gelu(values, approximate=True)


def local(
    inputs,
    cotangent,
    lengths,
    attn_scale,
    w_query,
    w_key,
    w_value,
    w_out,
    rel_table,
    ffn_scale,
    w_gate,
    w_up,
    w_down,
):
    seqs = lax.axis_size("seq")
    near_count = lax.axis_size("near")
    mp_count = lax.axis_size("mp")
    members = near_count * CORES
    sources = seqs * members
    tok_rows, model = inputs.shape
    seq_len = tok_rows * members
    own_rows = tok_rows // mp_count
    half_rows = seq_len // CORES
    shard = attn_scale.shape[0]
    table_rows, heads_mp = rel_table.shape
    buckets = table_rows * sources
    heads = heads_mp // members
    width = w_query.shape[1] // members
    hidden_width = w_gate.shape[1] // members

    near_at = lax.axis_index("near")
    core_at = lax.axis_index("core")
    mp_at = lax.axis_index("mp")
    member_at = near_at * CORES + core_at
    length = lax.dynamic_slice_in_dim(lengths, lax.axis_index("seq"), 1, 0)
    place = jnp.concatenate([length, jnp.reshape(core_at, (1,)).astype(jnp.int32)])

    def for_column(parts):
        return jnp.broadcast_to(parts[None], (seqs,) + parts.shape).reshape(
            (sources,) + parts.shape[1:]
        )

    def by_member(weight):
        return weight.reshape(weight.shape[0], members, -1)

    def scaled(weight, gain):
        low = weight.astype(LOW).astype(F32)
        return (low * gain.astype(LOW).astype(F32)[:, None]).astype(LOW)

    def over_mp(own, axis):
        shape = own.shape[:axis] + (mp_count,) + own.shape[axis:]
        blocks = lax.dynamic_update_index_in_dim(jnp.zeros(shape, own.dtype), own, mp_at, axis)
        moved = [(away, shifted(own, away)) for away in reversed(range(1, mp_count))]
        for away, block in moved:
            blocks = lax.dynamic_update_index_in_dim(blocks, block, mp_at ^ away, axis)
        return blocks

    def shifted(block, away):
        return lax.ppermute(block, "mp", [(i, i ^ away) for i in range(mp_count)])

    def in_near_order(own, moved):
        return jnp.stack(
            [jnp.where(near_at == 0, own, moved), jnp.where(near_at == 0, moved, own)], 0
        )

    def near_block_rows(block):
        own = lax.dynamic_slice_in_dim(block, mp_at * own_rows, own_rows, 0)
        moved = over_mp(swap(own, "near"), 0).reshape(tok_rows, model)
        return in_near_order(block, moved).reshape(half_rows, model)

    def gather_rows(near):
        blocks = [(0, near)] + [(away, shifted(near, away)) for away in range(1, mp_count)]
        shape = (near_count, mp_count, own_rows, model)
        mine, other = jnp.zeros(shape, near.dtype), jnp.zeros(shape, near.dtype)
        for away, block in blocks:
            at = mp_at ^ away
            mine = lax.dynamic_update_index_in_dim(mine, block, at, 1)
            other = lax.dynamic_update_index_in_dim(other, swap(block, "core"), at, 1)
        return mine.reshape(half_rows, model), other.reshape(half_rows, model)

    def sum_cores(mine, other):
        mine = mine.reshape(near_count, mp_count, own_rows, model)
        other = other.astype(LOW).reshape(near_count, mp_count, own_rows, model)
        sums = []
        for away in reversed(range(mp_count)):
            at = mp_at ^ away
            arrived = swap(lax.dynamic_index_in_dim(other, at, 1, keepdims=False), "core")
            kept = lax.dynamic_index_in_dim(mine, at, 1, keepdims=False)
            sums.append(kept.astype(F32) + arrived.astype(F32))
        return sums

    def send_mp(sums):
        last = len(sums) - 1
        moved = [shifted(rows.astype(LOW), last - i) for i, rows in enumerate(sums[:-1])]
        return moved, sums[-1]

    def sum_mp(sums):
        moved, kept = send_mp(sums)
        return sum((piece.astype(F32) for piece in moved), kept)

    def sum_near(pair):
        sent = jnp.where(near_at == 0, pair[1], pair[0]).astype(LOW)
        kept = jnp.where(near_at == 0, pair[0], pair[1])
        return kept + swap(sent, "near").astype(F32)

    def sum_near_both(pair):
        low = pair.astype(LOW)
        moved = swap(low, "near")
        return low.astype(F32) + moved.astype(F32), moved

    def near_pair(rows):
        blocks = rows.reshape(near_count, mp_count, own_rows, model)
        return lax.dynamic_index_in_dim(blocks, mp_at, 1, keepdims=False)

    def here(pair):
        return lax.dynamic_index_in_dim(pair, near_at, 0, keepdims=False)

    attn_parts = jnp.moveaxis(
        jnp.concatenate(
            [
                by_member(scaled(w_query, attn_scale)),
                by_member(scaled(w_key, attn_scale)),
                by_member(scaled(w_value, attn_scale)),
                by_member(w_out.T.astype(LOW)),
            ],
            2,
        ),
        1,
        0,
    )
    table_parts = rel_table.astype(LOW).reshape(table_rows, members, heads)
    table_parts = jnp.moveaxis(table_parts, 1, 0).reshape(members, 1, table_rows * heads)
    table_parts = jnp.pad(
        table_parts, ((0, 0), (0, EXTRA - 1), (0, 4 * width - table_rows * heads))
    )
    gate_up_parts = for_column(
        jnp.moveaxis(
            jnp.concatenate(
                [by_member(scaled(w_gate, ffn_scale)), by_member(scaled(w_up, ffn_scale))], 2
            ),
            1,
            0,
        )
    )
    down_parts = for_column(w_down.astype(LOW).reshape(members, hidden_width, shard))

    attn_got = exchange(for_column(jnp.concatenate([attn_parts, table_parts], 1)), COLUMN)
    attn_weights = attn_got[:, :shard].reshape(model, 4 * width)
    qkv_weight = attn_weights[:, : 3 * width]
    out_weight_t = attn_weights[:, 3 * width :]
    table = attn_got[:, shard, : table_rows * heads].reshape(buckets, heads)
    table = jnp.pad(table.T, ((0, 8 - heads), (0, 0)))

    mine_inputs = near_block_rows(inputs)
    mine_values = mine_inputs.astype(F32)
    mine_normed = (mine_values * rms(mine_values)).astype(LOW)
    normed_rows = jnp.concatenate([mine_normed, swap(mine_normed, "core")], 0)
    row_valid = (member_at * tok_rows + lax.iota(jnp.int32, tok_rows) < length)[:, None]
    later_cotangent = after(cotangent, mine_inputs)
    masked = jnp.where(row_valid, later_cotangent, jnp.zeros_like(cotangent))
    mine_grad = near_block_rows(masked)
    other_grad = swap(mine_grad, "core")

    normed_rows = after(normed_rows, gate_up_parts, down_parts)
    down_got = exchange(after(down_parts, attn_got), COLUMN)
    down_weight = jnp.moveaxis(down_got, 0, 1).reshape(hidden_width, model)

    qkv = rows_dot(normed_rows, qkv_weight).astype(LOW)
    attended, prob = attention_forward(qkv, table, place, heads, tok_rows)
    attended = after(attended, mine_grad, other_grad)
    mixed, mixed_moved = sum_near_both(
        after(
            sum_mp(
                sum_cores(
                    contract_cols(attended[:half_rows], out_weight_t),
                    contract_cols(attended[half_rows:], out_weight_t),
                )
            ),
            down_got,
        )
    )
    gate_up_weight = exchange(after(gate_up_parts, mixed_moved), COLUMN).reshape(model, 2 * hidden_width)

    pair_inputs = near_pair(after(mine_inputs, normed_rows)).astype(F32)
    pair_cotangent = near_pair(mine_grad).astype(F32)
    after_attn = pair_inputs + mixed
    inv_two = rms(after_attn)
    normed_two = after_attn * inv_two
    halves = gather_rows(normed_two.astype(LOW))

    grads = (mine_grad, other_grad)
    ups, gelus, acts = [], [], []
    for rows in halves:
        gate_up = rows_dot(rows, gate_up_weight)
        gelus.append(jax.vjp(gelu_tanh, gate_up[:, :hidden_width]))
        ups.append(gate_up[:, hidden_width:])
        acts.append((gelus[-1][0] * ups[-1]).astype(LOW))
    d_down_w = (contract_rows(acts[0], grads[0]) + contract_rows(acts[1], grads[1])).astype(LOW)
    d_gate_ups, d_norms = [], []
    for grad, up_pre, (gelu_value, gelu_pull) in zip(grads, ups, gelus):
        d_hidden = contract_cols(after(grad, d_down_w), down_weight)
        (d_gate_pre,) = gelu_pull(d_hidden * up_pre)
        d_gate_ups.append(
            jnp.concatenate([d_gate_pre.astype(LOW), (d_hidden * gelu_value).astype(LOW)], 1)
        )
        d_norms.append(contract_cols(d_gate_ups[-1], gate_up_weight))
    inner_cores = sum_cores(*d_norms)
    ffn_cores = sum_cores(*[rows_dot(after(act, *inner_cores), down_weight) for act in acts])
    d_gate_ups = [after(grad, *d_norms) for grad in d_gate_ups]

    def to_owners(grad):
        return exchange(grad, COLUMN)

    def of_owner(got):
        parts = got.reshape((seqs, members) + got.shape[1:]).astype(F32)
        return jnp.moveaxis(jnp.sum(parts, axis=0), 0, 1)

    def flat(parts):
        return parts.reshape(shard, -1)

    def by_rows(got):
        parts = got.reshape((seqs, members) + got.shape[1:]).astype(F32)
        return jnp.sum(parts, axis=0).reshape(-1, shard)

    d_down = to_owners(jnp.moveaxis(d_down_w.reshape(hidden_width, sources, shard), 1, 0))
    inner_two, inner_moved = sum_near_both(after(sum_mp(inner_cores), d_down, *ffn_cores))
    d_gate_up_w = (
        contract_rows(halves[0], d_gate_ups[0]) + contract_rows(halves[1], d_gate_ups[1])
    ).astype(LOW)
    d_gate_up = to_owners(after(d_gate_up_w, inner_moved).reshape(sources, shard, -1))

    pair_first = (
        lax.broadcasted_iota(jnp.int32, (near_count, own_rows, 1), 0) * (CORES * tok_rows)
        + lax.broadcasted_iota(jnp.int32, (near_count, own_rows, 1), 1)
        + (core_at * tok_rows + mp_at * own_rows)
    )
    pair_valid = pair_first < length
    grad_one = pair_cotangent + norm_grad(inner_two, normed_two, inv_two)
    mine_one, other_one = gather_rows(grad_one.astype(LOW))
    d_attended = jnp.concatenate(
        [rows_dot(mine_one, out_weight_t), rows_dot(other_one, out_weight_t)], 0
    ).astype(LOW)
    d_qkv, d_table = attention_backward(prob, d_attended, qkv, place, heads, tok_rows, buckets)
    inner_cores = sum_cores(
        contract_cols(d_qkv[:half_rows], qkv_weight), contract_cols(d_qkv[half_rows:], qkv_weight)
    )
    ffn_moved, ffn_kept = send_mp([after(rows, mine_one) for rows in ffn_cores])
    ffn_moved = [after(rows, d_qkv) for rows in ffn_moved]
    inner_one = sum_near(after(sum_mp(inner_cores), d_gate_up))
    table_sent = d_table[:, :heads].astype(LOW).reshape(sources, 1, table_rows * heads)
    table_sent = jnp.pad(
        table_sent, ((0, 0), (0, EXTRA - 1), (0, 3 * width - table_rows * heads))
    )
    d_qkv_w = contract_rows(normed_rows, d_qkv).astype(LOW).reshape(sources, shard, -1)
    d_qkv_got = to_owners(after(jnp.concatenate([d_qkv_w, table_sent], 1), d_gate_up))
    later_attended = after(attended, inner_cores[0])
    d_out = contract_rows(later_attended[:half_rows], mine_one) + contract_rows(
        later_attended[half_rows:], other_one
    )
    d_out = jnp.moveaxis(d_out.astype(LOW).reshape(width, sources, shard), 1, 0)
    d_out = to_owners(after(d_out, d_qkv_got))

    own_inputs = here(pair_inputs)
    normed_one = own_inputs * rms(own_inputs)
    grad_input = here(grad_one) + norm_grad(inner_one, normed_one, rms(own_inputs))
    d_inputs = over_mp(grad_input.astype(LOW), 0).reshape(tok_rows, model)
    ffn_pair = sum((piece.astype(F32) for piece in ffn_moved), ffn_kept)
    after_ffn = here(after_attn) + sum_near(after(ffn_pair, inner_one))
    own_out = jnp.where(here(pair_valid), after_ffn, 0.0).astype(LOW)
    layer_out = over_mp(own_out, 0).reshape(tok_rows, model)

    g_gate_up = of_owner(after(d_gate_up, inner_cores[0]))
    g_gate, g_up = flat(g_gate_up[:, :, :hidden_width]), flat(g_gate_up[:, :, hidden_width:])
    got_qkv = of_owner(d_qkv_got)
    g_query, g_key, g_value = (
        flat(got_qkv[:shard, :, i * width : (i + 1) * width]) for i in range(3)
    )
    d_rel_table = got_qkv[shard, :, : table_rows * heads].reshape(members, table_rows, heads)
    d_rel_table = jnp.moveaxis(d_rel_table, 0, 1).reshape(table_rows, heads_mp)

    def gain_grad(pairs):
        return sum(jnp.sum(w.astype(LOW).astype(F32) * g, axis=1) for w, g in pairs)

    gains = jnp.stack(
        [
            gain_grad([(w_query, g_query), (w_key, g_key), (w_value, g_value)]),
            gain_grad([(w_gate, g_gate), (w_up, g_up)]),
        ]
    )
    gains = sum((shifted(gains, away) for away in range(1, mp_count)), gains)
    attn_gain = attn_scale.astype(LOW).astype(F32)[:, None]
    ffn_gain = ffn_scale.astype(LOW).astype(F32)[:, None]
    return (
        layer_out,
        d_inputs,
        gains[0],
        g_query * attn_gain,
        g_key * attn_gain,
        g_value * attn_gain,
        by_rows(d_out),
        d_rel_table,
        gains[1],
        g_gate * ffn_gain,
        g_up * ffn_gain,
        by_rows(after(d_down, d_qkv)),
    )


def solution(mesh):
    fsdp, mp = mesh.shape["fsdp"], mesh.shape["mp"]

    def run(*args):
        seqs = args[2].shape[0]
        members = fsdp // seqs
        inner = Mesh(
            mesh.devices.reshape(seqs, members // CORES, CORES, mp), ("seq", "near", "core", "mp")
        )
        rows, columns, first = P(COLUMN, None), P("mp", COLUMN), P(COLUMN)
        both = P(COLUMN, "mp")
        in_specs = (
            rows, rows, P(), first, both, both, both, columns, both, first, both, both, columns,
        )
        out_specs = (
            rows, rows, first, both, both, both, columns, both, first, both, both, columns,
        )
        return jax.shard_map(
            local, mesh=inner, in_specs=in_specs, out_specs=out_specs, check_vma=False
        )(*args)

    return run
```

profile of v0, /device:TPU:0, one launch (start us, length us, event | category | flops | bytes accessed | tf_op | source)
XLA Modules:
  0.0 522.9 jit_solution(4707839206340645263)
XLA Ops:
  21.2 5.7 %collective-permute-done.1 = bf16[64,2048]{1,0:T(8,128)(2,1)S(1)} collective-permute-done((bf16[64,2048]{1,0:T(8,128)(2,1)}, bf16[64,2048]{1,0:T(8,128)(2,1)S(1)}, u32[]{:S(2)}, u32[]{:S(2)}) %collective-permute-start.1) | collective-permute-done | bytes 262176 | tf_op jit(solution)/shard_map/ppermute | solution.py:348
  26.9 5.1 collective-permute-done.2
  38.4 18.5 %collective-permute-done.5 = bf16[64,2048]{1,0:T(8,128)(2,1)S(1)} collective-permute-done((bf16[64,2048]{1,0:T(8,128)(2,1)S(1)}, bf16[64,2048]{1,0:T(8,128)(2,1)S(1)}, u32[]{:S(2)}, u32[]{:S(2)}) %collective-permute-start.5) | collective-permute-done | bytes 262176 | tf_op jit(solution)/shard_map/ppermute | solution.py:258
  60.4 6.5 %collective-permute-done.6 = bf16[64,2048]{1,0:T(8,128)(2,1)S(1)} collective-permute-done((bf16[64,2048]{1,0:T(8,128)(2,1)S(1)}, bf16[64,2048]{1,0:T(8,128)(2,1)S(1)}, u32[]{:S(2)}, u32[]{:S(2)}) %collective-permute-start.6) | collective-permute-done | bytes 262176 | tf_op jit(solution)/shard_map/ppermute | solution.py:348
  83.3 4.9 pad_maximum_fusion
  96.6 7.5 %attention_forward.1 = (bf16[1024,128]{1,0:T(8,128)(2,1)S(1)}, bf16[2,1024,1024]{2,1,0:T(8,128)(2,1)S(1)}) custom-call(s32[2]{0:T(128)S(1)} %pad_add_fusion.place_ref, bf16[1024,384]{1,0:T(8,128)(2,1)S(1)} %convolution_convert_fusion.4.qkv_ref, bf16[8,32]{1,0:T(8,128)(2,1)S(1)} %pad.13.table_ref), custom_call_target="tpu_custom_call" | custom-call | flops 536870912 | bytes 4194304 | tf_op jit(solution)/shard_map/attention_forward/pallas_call | solution.py:117
  108.2 5.9 %all-to-all-start.1 = ((bf16[8,320,256]{2,1,0:T(8,128)(2,1)}), bf16[8,320,256]{2,1,0:T(8,128)(2,1)S(1)}, u32[]{:S(2)}, u32[]{:S(2)}) async-start(bf16[8,320,256]{2,1,0:T(8,128)(2,1)} %bitcast.410), calls=%async_computation.1 | async-start | bytes 2621440 | tf_op jit(solution)/shard_map/all_to_all | solution.py:254
  123.5 12.2 %collective-permute-done.12 = bf16[2,64,2048]{2,1,0:T(8,128)(2,1)S(1)} collective-permute-done((bf16[2,64,2048]{2,1,0:T(8,128)(2,1)S(1)}, bf16[2,64,2048]{2,1,0:T(8,128)(2,1)S(1)}, u32[]{:S(2)}, u32[]{:S(2)}) %collective-permute-start.12) | collective-permute-done | bytes 524320 | tf_op jit(solution)/shard_map/ppermute | solution.py:348
  135.7 10.6 %collective-permute-done.14 = bf16[2,64,2048]{2,1,0:T(8,128)(2,1)S(1)} collective-permute-done((bf16[2,64,2048]{2,1,0:T(8,128)(2,1)S(1)}, bf16[2,64,2048]{2,1,0:T(8,128)(2,1)S(1)}, u32[]{:S(2)}, u32[]{:S(2)}) %collective-permute-start.14) | collective-permute-done | bytes 524320 | tf_op jit(solution)/shard_map/ppermute | solution.py:348
  148.5 12.2 %collective-permute-done.17 = bf16[2,64,2048]{2,1,0:T(8,128)(2,1)S(1)} collective-permute-done((bf16[2,64,2048]{2,1,0:T(8,128)(2,1)S(1)}, bf16[2,64,2048]{2,1,0:T(8,128)(2,1)S(1)}, u32[]{:S(2)}, u32[]{:S(2)}) %collective-permute-start.17) | collective-permute-done | bytes 524320 | tf_op jit(solution)/shard_map/ppermute | solution.py:258
  161.5 4.7 all-to-all-start.2
  173.1 10.0 %collective-permute-done.18 = bf16[2,64,2048]{2,1,0:T(8,128)(2,1)S(1)} collective-permute-done((bf16[2,64,2048]{2,1,0:T(8,128)(2,1)S(1)}, bf16[2,64,2048]{2,1,0:T(8,128)(2,1)S(1)}, u32[]{:S(2)}, u32[]{:S(2)}) %collective-permute-start.18) | collective-permute-done | bytes 524320 | tf_op jit(solution)/shard_map/ppermute | solution.py:348
  183.1 12.0 %collective-permute-done.19 = bf16[2,64,2048]{2,1,0:T(8,128)(2,1)S(1)} collective-permute-done((bf16[2,64,2048]{2,1,0:T(8,128)(2,1)S(1)}, bf16[2,64,2048]{2,1,0:T(8,128)(2,1)S(1)}, u32[]{:S(2)}, u32[]{:S(2)}) %collective-permute-start.19) | collective-permute-done | bytes 524320 | tf_op jit(solution)/shard_map/ppermute | solution.py:348
  201.0 25.6 %all-to-all-done.2 = bf16[8,256,640]{2,1,0:T(8,128)(2,1)} async-done(((bf16[8,256,640]{2,1,0:T(8,128)(2,1)}), bf16[8,256,640]{2,1,0:T(8,128)(2,1)}, u32[]{:S(2)}, u32[]{:S(2)}) %all-to-all-start.2) | async-done | bytes 2621472 | tf_op jit(solution)/shard_map/all_to_all | solution.py:254
  255.0 12.2 %fusion.77 = f32[512,2048]{1,0:T(8,128)S(1)} fusion(bf16[512,640]{1,0:T(8,128)(2,1)S(1)} %pad_maximum_fusion.3, bf16[2048,640]{1,0:T(8,128)(2,1)} %bitcast.59), kind=kOutput, calls=%fused_computation.235 | convolution fusion | flops 1342177280 | bytes 7471104 | tf_op jit(solution)/shard_map/dot_general | solution.py:270
  285.7 10.2 %collective-permute-done.31 = bf16[2,64,2048]{2,1,0:T(8,128)(2,1)} collective-permute-done((bf16[2,64,2048]{2,1,0:T(8,128)(2,1)}, bf16[2,64,2048]{2,1,0:T(8,128)(2,1)}, u32[]{:S(2)}, u32[]{:S(2)}) %collective-permute-start.31) | collective-permute-done | bytes 524320 | tf_op jit(solution)/shard_map/ppermute | solution.py:348
  318.7 10.2 %collective-permute-done.36 = bf16[2,64,2048]{2,1,0:T(8,128)(2,1)S(1)} collective-permute-done((bf16[2,64,2048]{2,1,0:T(8,128)(2,1)S(1)}, bf16[2,64,2048]{2,1,0:T(8,128)(2,1)S(1)}, u32[]{:S(2)}, u32[]{:S(2)}) %collective-permute-start.36) | collective-permute-done | bytes 524320 | tf_op jit(solution)/shard_map/ppermute | solution.py:258
  334.6 4.9 add_convert_fusion
  349.5 8.6 %collective-permute-done.38 = bf16[2,64,2048]{2,1,0:T(8,128)(2,1)S(1)} collective-permute-done((bf16[2,64,2048]{2,1,0:T(8,128)(2,1)}, bf16[2,64,2048]{2,1,0:T(8,128)(2,1)S(1)}, u32[]{:S(2)}, u32[]{:S(2)}) %collective-permute-start.38) | collective-permute-done | bytes 524320 | tf_op jit(solution)/shard_map/ppermute | solution.py:348
  371.4 12.5 %attention_backward.1 = (bf16[1024,384]{1,0:T(8,128)(2,1)S(1)}, f32[32,128]{1,0:T(8,128)S(1)}) custom-call(s32[2]{0:T(128)S(1)} %pad_add_fusion.place_ref, bf16[2,1024,1024]{2,1,0:T(8,128)(2,1)S(1)} %copy-done.1, bf16[1024,128]{1,0:T(8,128)(2,1)S(1)} %pad_maximum_fusion.5.do_ref, bf16[1024,384]{1,0:T(8,128)(2,1)S(1)} %convolution_convert_fusion.4.qkv_ref), custom_call_target="tpu_custom_call" | custom-call | flops 4294967296 | bytes 4194304 | tf_op jit(solution)/shard_map/attention_backward/pallas_call | solution.py:217
  407.2 10.0 %collective-permute-done.49 = bf16[2,64,2048]{2,1,0:T(8,128)(2,1)S(1)} collective-permute-done((bf16[2,64,2048]{2,1,0:T(8,128)(2,1)S(1)}, bf16[2,64,2048]{2,1,0:T(8,128)(2,1)S(1)}, u32[]{:S(2)}, u32[]{:S(2)}) %collective-permute-start.49) | collective-permute-done | bytes 524320 | tf_op jit(solution)/shard_map/ppermute | solution.py:348
  417.2 10.6 %collective-permute-done.51 = bf16[2,64,2048]{2,1,0:T(8,128)(2,1)S(1)} collective-permute-done((bf16[2,64,2048]{2,1,0:T(8,128)(2,1)S(1)}, bf16[2,64,2048]{2,1,0:T(8,128)(2,1)S(1)}, u32[]{:S(2)}, u32[]{:S(2)}) %collective-permute-start.51) | collective-permute-done | bytes 524320 | tf_op jit(solution)/shard_map/ppermute | solution.py:348
  455.6 10.1 %collective-permute-done.54 = bf16[64,2048]{1,0:T(8,128)(2,1)} collective-permute-done((bf16[64,2048]{1,0:T(8,128)(2,1)}, bf16[64,2048]{1,0:T(8,128)(2,1)}, u32[]{:S(2)}, u32[]{:S(2)}) %collective-permute-start.54) | collective-permute-done | bytes 262176 | tf_op jit(solution)/shard_map/ppermute | solution.py:258
  486.2 5.5 %collective-permute-done.56 = bf16[64,2048]{1,0:T(8,128)(2,1)S(1)} collective-permute-done((bf16[64,2048]{1,0:T(8,128)(2,1)}, bf16[64,2048]{1,0:T(8,128)(2,1)S(1)}, u32[]{:S(2)}, u32[]{:S(2)}) %collective-permute-start.56) | collective-permute-done | bytes 262176 | tf_op jit(solution)/shard_map/ppermute | solution.py:348
  (410 shorter events, 284.2 us)
Async XLA Ops:
  11.3 79.8 %all-to-all-start = ((bf16[8,264,512]{2,1,0:T(8,128)(2,1)}), bf16[8,264,512]{2,1,0:T(8,128)(2,1)S(1)}, u32[]{:S(2)}, u32[]{:S(2)}) async-start(bf16[8,264,512]{2,1,0:T(8,128)(2,1)} %bitcast.28), calls=%async_computation | async-start | bytes 4325376 | tf_op jit(solution)/shard_map/all_to_all | solution.py:254
  38.4 45.0 %collective-permute-start.4 = (bf16[512,2048]{1,0:T(8,128)(2,1)}, bf16[512,2048]{1,0:T(8,128)(2,1)}, u32[]{:S(2)}, u32[]{:S(2)}) collective-permute-start(bf16[512,2048]{1,0:T(8,128)(2,1)} %multiply_convert_fusion), channel_id=1, source_target_pairs={{0,4},{4,0},{1,5},{5,1},{2,6},{6,2},{3,7},{7,3},{8,12},{12,8},{9,1... | collective-permute-start | bytes 6291464 | tf_op jit(solution)/shard_map/ppermute | solution.py:258
  74.0 32.1 %collective-permute-start.9 = (bf16[512,2048]{1,0:T(8,128)(2,1)}, bf16[512,2048]{1,0:T(8,128)(2,1)}, u32[]{:S(2)}, u32[]{:S(2)}) collective-permute-start(bf16[512,2048]{1,0:T(8,128)(2,1)} %bitcast.38), channel_id=1, source_target_pairs={{0,4},{4,0},{1,5},{5,1},{2,6},{6,2},{3,7},{7,3},{8,12},{12,8},{9,1... | collective-permute-start | bytes 6291464 | tf_op jit(solution)/shard_map/ppermute | solution.py:258
  108.2 38.6 %all-to-all-start.1 = ((bf16[8,320,256]{2,1,0:T(8,128)(2,1)}), bf16[8,320,256]{2,1,0:T(8,128)(2,1)S(1)}, u32[]{:S(2)}, u32[]{:S(2)}) async-start(bf16[8,320,256]{2,1,0:T(8,128)(2,1)} %bitcast.410), calls=%async_computation.1 | async-start | bytes 2621440 | tf_op jit(solution)/shard_map/all_to_all | solution.py:254
  121.7 24.6 %collective-permute-start.14 = (bf16[2,64,2048]{2,1,0:T(8,128)(2,1)S(1)}, bf16[2,64,2048]{2,1,0:T(8,128)(2,1)S(1)}, u32[]{:S(2)}, u32[]{:S(2)}) collective-permute-start(bf16[2,64,2048]{2,1,0:T(8,128)(2,1)S(1)} %get-tuple-element.151), channel_id=1, source_target_pairs={{0,2},{1,3},{2,0},{3,1},{4,6},{5,7},{6,4},{7,5},{8,10},{9,11},{10,... | collective-permute-start | bytes 1572872 | tf_op jit(solution)/shard_map/ppermute | solution.py:348
  122.9 23.4 %collective-permute-start.16 = (bf16[2,64,2048]{2,1,0:T(8,128)(2,1)S(1)}, bf16[2,64,2048]{2,1,0:T(8,128)(2,1)S(1)}, u32[]{:S(2)}, u32[]{:S(2)}) collective-permute-start(bf16[2,64,2048]{2,1,0:T(8,128)(2,1)S(1)} %get-tuple-element.150), channel_id=1, source_target_pairs={{0,1},{1,0},{2,3},{3,2},{4,5},{5,4},{6,7},{7,6},{8,9},{9,8},{10,11... | collective-permute-start | bytes 1572872 | tf_op jit(solution)/shard_map/ppermute | solution.py:348
  161.5 65.1 %all-to-all-start.2 = ((bf16[8,256,640]{2,1,0:T(8,128)(2,1)}), bf16[8,256,640]{2,1,0:T(8,128)(2,1)}, u32[]{:S(2)}, u32[]{:S(2)}) async-start(bf16[8,256,640]{2,1,0:T(8,128)(2,1)} %bitcast.391), calls=%async_computation.2 | async-start | bytes 5242880 | tf_op jit(solution)/shard_map/all_to_all | solution.py:254
  169.8 25.3 %collective-permute-start.19 = (bf16[2,64,2048]{2,1,0:T(8,128)(2,1)S(1)}, bf16[2,64,2048]{2,1,0:T(8,128)(2,1)S(1)}, u32[]{:S(2)}, u32[]{:S(2)}) collective-permute-start(bf16[2,64,2048]{2,1,0:T(8,128)(2,1)S(1)} %get-tuple-element.138), channel_id=1, source_target_pairs={{0,2},{1,3},{2,0},{3,1},{4,6},{5,7},{6,4},{7,5},{8,10},{9,11},{10,... | collective-permute-start | bytes 1572872 | tf_op jit(solution)/shard_map/ppermute | solution.py:348
  171.8 23.4 %collective-permute-start.20 = (bf16[2,64,2048]{2,1,0:T(8,128)(2,1)S(1)}, bf16[2,64,2048]{2,1,0:T(8,128)(2,1)S(1)}, u32[]{:S(2)}, u32[]{:S(2)}) collective-permute-start(bf16[2,64,2048]{2,1,0:T(8,128)(2,1)S(1)} %get-tuple-element.138), channel_id=1, source_target_pairs={{0,3},{1,2},{2,1},{3,0},{4,7},{5,6},{6,5},{7,4},{8,11},{9,10},{10,... | collective-permute-start | bytes 1572872 | tf_op jit(solution)/shard_map/ppermute | solution.py:348
  254.2 27.6 %collective-permute-start.28 = (bf16[2,64,2048]{2,1,0:T(8,128)(2,1)}, bf16[2,64,2048]{2,1,0:T(8,128)(2,1)}, u32[]{:S(2)}, u32[]{:S(2)}) collective-permute-start(bf16[2,64,2048]{2,1,0:T(8,128)(2,1)} %get-tuple-element.162), channel_id=1, source_target_pairs={{0,4},{4,0},{1,5},{5,1},{2,6},{6,2},{3,7},{7,3},{8,12},{12,8},{9,1... | collective-permute-start | bytes 1572872 | tf_op jit(solution)/shard_map/ppermute | solution.py:258
  271.3 24.6 %collective-permute-start.31 = (bf16[2,64,2048]{2,1,0:T(8,128)(2,1)}, bf16[2,64,2048]{2,1,0:T(8,128)(2,1)}, u32[]{:S(2)}, u32[]{:S(2)}) collective-permute-start(bf16[2,64,2048]{2,1,0:T(8,128)(2,1)} %get-tuple-element.147), channel_id=1, source_target_pairs={{0,2},{1,3},{2,0},{3,1},{4,6},{5,7},{6,4},{7,5},{8,10},{9,11},{10,... | collective-permute-start | bytes 1572872 | tf_op jit(solution)/shard_map/ppermute | solution.py:348
  272.6 23.4 %collective-permute-start.32 = (bf16[2,64,2048]{2,1,0:T(8,128)(2,1)}, bf16[2,64,2048]{2,1,0:T(8,128)(2,1)}, u32[]{:S(2)}, u32[]{:S(2)}) collective-permute-start(bf16[2,64,2048]{2,1,0:T(8,128)(2,1)} %get-tuple-element.146), channel_id=1, source_target_pairs={{0,1},{1,0},{2,3},{3,2},{4,5},{5,4},{6,7},{7,6},{8,9},{9,8},{10,11... | collective-permute-start | bytes 1572872 | tf_op jit(solution)/shard_map/ppermute | solution.py:348
  277.5 37.5 %all-to-all-start.3 = ((bf16[8,320,256]{2,1,0:T(8,128)(2,1)}), bf16[8,320,256]{2,1,0:T(8,128)(2,1)}, u32[]{:S(2)}, u32[]{:S(2)}) async-start(bf16[8,320,256]{2,1,0:T(8,128)(2,1)} %bitcast.411), calls=%async_computation.3 | async-start | bytes 2621440 | tf_op jit(solution)/shard_map/all_to_all | solution.py:254
  333.8 24.2 %collective-permute-start.38 = (bf16[2,64,2048]{2,1,0:T(8,128)(2,1)}, bf16[2,64,2048]{2,1,0:T(8,128)(2,1)S(1)}, u32[]{:S(2)}, u32[]{:S(2)}) collective-permute-start(bf16[2,64,2048]{2,1,0:T(8,128)(2,1)} %get-tuple-element.133), channel_id=1, source_target_pairs={{0,2},{1,3},{2,0},{3,1},{4,6},{5,7},{6,4},{7,5},{8,10},{9,11},{10,... | collective-permute-start | bytes 1572872 | tf_op jit(solution)/shard_map/ppermute | solution.py:348
  339.5 26.2 %collective-permute-start.41 = (bf16[2,64,2048]{2,1,0:T(8,128)(2,1)}, bf16[2,64,2048]{2,1,0:T(8,128)(2,1)}, u32[]{:S(2)}, u32[]{:S(2)}) collective-permute-start(bf16[2,64,2048]{2,1,0:T(8,128)(2,1)} %get-tuple-element.133), channel_id=1, source_target_pairs={{0,4},{4,0},{1,5},{5,1},{2,6},{6,2},{3,7},{7,3},{8,12},{12,8},{9,1... | collective-permute-start | bytes 1572872 | tf_op jit(solution)/shard_map/ppermute | solution.py:258
  340.8 87.4 %all-to-all-start.4 = ((bf16[8,256,640]{2,1,0:T(8,128)(2,1)}), bf16[8,256,640]{2,1,0:T(8,128)(2,1)}, u32[]{:S(2)}, u32[]{:S(2)}) async-start(bf16[8,256,640]{2,1,0:T(8,128)(2,1)} %bitcast.373), calls=%async_computation.4 | async-start | bytes 5242880 | tf_op jit(solution)/shard_map/all_to_all | solution.py:254
  362.2 24.9 %collective-permute-start.40 = (bf16[2,64,2048]{2,1,0:T(8,128)(2,1)}, bf16[2,64,2048]{2,1,0:T(8,128)(2,1)S(1)}, u32[]{:S(2)}, u32[]{:S(2)}) collective-permute-start(bf16[2,64,2048]{2,1,0:T(8,128)(2,1)} %get-tuple-element.59), channel_id=1, source_target_pairs={{0,3},{1,2},{2,1},{3,0},{4,7},{5,6},{6,5},{7,4},{8,11},{9,10},{10,... | collective-permute-start | bytes 1572872 | tf_op jit(solution)/shard_map/ppermute | solution.py:348
  363.7 23.8 %collective-permute-start.45 = (bf16[2,64,2048]{2,1,0:T(8,128)(2,1)}, bf16[2,64,2048]{2,1,0:T(8,128)(2,1)}, u32[]{:S(2)}, u32[]{:S(2)}) collective-permute-start(bf16[2,64,2048]{2,1,0:T(8,128)(2,1)} %get-tuple-element.63), channel_id=1, source_target_pairs={{0,2},{1,3},{2,0},{3,1},{4,6},{5,7},{6,4},{7,5},{8,10},{9,11},{10,... | collective-permute-start | bytes 1572872 | tf_op jit(solution)/shard_map/ppermute | solution.py:348
  363.7 23.9 %collective-permute-start.46 = (bf16[2,64,2048]{2,1,0:T(8,128)(2,1)}, bf16[2,64,2048]{2,1,0:T(8,128)(2,1)}, u32[]{:S(2)}, u32[]{:S(2)}) collective-permute-start(bf16[2,64,2048]{2,1,0:T(8,128)(2,1)} %get-tuple-element.65), channel_id=1, source_target_pairs={{0,1},{1,0},{2,3},{3,2},{4,5},{5,4},{6,7},{7,6},{8,9},{9,8},{10,11... | collective-permute-start | bytes 1572872 | tf_op jit(solution)/shard_map/ppermute | solution.py:348
  403.3 24.5 %collective-permute-start.51 = (bf16[2,64,2048]{2,1,0:T(8,128)(2,1)S(1)}, bf16[2,64,2048]{2,1,0:T(8,128)(2,1)S(1)}, u32[]{:S(2)}, u32[]{:S(2)}) collective-permute-start(bf16[2,64,2048]{2,1,0:T(8,128)(2,1)S(1)} %get-tuple-element.141), channel_id=1, source_target_pairs={{0,2},{1,3},{2,0},{3,1},{4,6},{5,7},{6,4},{7,5},{8,10},{9,11},{10,... | collective-permute-start | bytes 1572872 | tf_op jit(solution)/shard_map/ppermute | solution.py:348
  403.4 24.5 %collective-permute-start.53 = (bf16[2,64,2048]{2,1,0:T(8,128)(2,1)S(1)}, bf16[2,64,2048]{2,1,0:T(8,128)(2,1)S(1)}, u32[]{:S(2)}, u32[]{:S(2)}) collective-permute-start(bf16[2,64,2048]{2,1,0:T(8,128)(2,1)S(1)} %get-tuple-element.142), channel_id=1, source_target_pairs={{0,1},{1,0},{2,3},{3,2},{4,5},{5,4},{6,7},{7,6},{8,9},{9,8},{10,11... | collective-permute-start | bytes 1572872 | tf_op jit(solution)/shard_map/ppermute | solution.py:348
  428.3 67.6 %all-to-all-start.5 = ((bf16[8,264,384]{2,1,0:T(8,128)(2,1)}), bf16[8,264,384]{2,1,0:T(8,128)(2,1)}, u32[]{:S(2)}, u32[]{:S(2)}) async-start(bf16[8,264,384]{2,1,0:T(8,128)(2,1)} %fusion.4), calls=%async_computation.5 | async-start | bytes 3244032 | tf_op jit(solution)/shard_map/all_to_all | solution.py:254
  480.4 32.8 %collective-permute-start.58 = (bf16[64,2048]{1,0:T(8,128)(2,1)}, bf16[64,2048]{1,0:T(8,128)(2,1)}, u32[]{:S(2)}, u32[]{:S(2)}) collective-permute-start(bf16[64,2048]{1,0:T(8,128)(2,1)} %get-tuple-element.131), channel_id=1, source_target_pairs={{0,1},{1,0},{2,3},{3,2},{4,5},{5,4},{6,7},{7,6},{8,9},{9,8},{10,11... | collective-permute-start | bytes 786440 | tf_op jit(solution)/shard_map/ppermute | solution.py:348
  495.9 24.5 %all-to-all-start.6 = ((bf16[8,128,256]{2,1,0:T(8,128)(2,1)}), bf16[8,128,256]{2,1,0:T(8,128)(2,1)}, u32[]{:S(2)}, u32[]{:S(2)}) async-start(bf16[8,128,256]{2,1,0:T(8,128)(2,1)} %bitcast.372), calls=%async_computation.6 | async-start | bytes 1048576 | tf_op jit(solution)/shard_map/all_to_all | solution.py:254
  (106 other events, 916.0 us)
where the time goes:
time: 533 us; the launch traced here: 523 us
  waiting for transfers between devices  209 us (39%)
  starting transfers between devices  87.9 us (16%)
  local copies, waits for them, and re-layouts  82.2 us (15%)
  matrix products  66.4 us (12%)
  other arithmetic  55.3 us (10%)
  Pallas kernels  20 us (4%)
    ppermute x33, waiting for transfers between devices, shifted(): return lax.ppermute(block, 'mp', [(i, i ^ away) for i in range(mp_count)])  126 us
    ppermute x32, waiting for transfers between devices, swap(): return lax.ppermute(block, axis, [(0, 1), (1, 0)])  56.6 us
    ppermute x33, starting transfers between devices, shifted(): return lax.ppermute(block, 'mp', [(i, i ^ away) for i in range(mp_count)])  38.8 us
    all_to_all x7, starting transfers between devices, exchange(): return lax.all_to_all(blocks, axes, split_axis=0, concat_axis=0, tiled=True)  32.6 us
    dot_general x8, matrix products, contract_cols(): lax.dot_general(left, right, (((1,), (1,)), ((), ())), preferred_element_...  29 us
    unnamed x130, local copies, waits for them, and re-layouts  29 us
    all_to_all x7, waiting for transfers between devices, exchange(): return lax.all_to_all(blocks, axes, split_axis=0, concat_axis=0, tiled=True)  25.6 us
    dot_general x7, matrix products, contract_rows(): lax.dot_general(left, right, (((0,), (0,)), ((), ())), preferred_element_...  20.3 us
  transfers between devices with their start and end apart: 72, of which 28 were waited for; matrix products, arithmetic and copies ran while one was open for 30% of the time, Pallas kernels for 4%

commit v1 on v0

--- a/solution.py
+++ b/solution.py
@@ -67,10 +67,14 @@
 
     @pl.when(step == 0)
     def _():
-        one_hot = bucket_onehot(table_ref.shape[1], seq_len).astype(F32).astype(LOW)
-        lines = jnp.dot(table_ref[...], one_hot, preferred_element_type=F32)
+        one_hot = bucket_onehot(table_ref.shape[0], seq_len)
+        table = table_ref[...].astype(F32)
+        column = lax.broadcasted_iota(jnp.int32, table.shape, 1)
         for head in range(heads):
-            line = jnp.broadcast_to(lines[head : head + 1], (SKEW, span))
+            here = column == place_ref[2] * heads + head
+            levels = jnp.sum(jnp.where(here, table, 0.0), axis=1, keepdims=True)
+            line = jnp.sum(jnp.where(one_hot, levels, 0.0), axis=0, keepdims=True)
+            line = jnp.broadcast_to(line, (SKEW, span))
             skew_ref[head] = pltpu.roll(line, span - SKEW, 1, stride=1, stride_axis=0)
 
     row = lax.broadcasted_iota(jnp.int32, (1, rows), 1)
@@ -246,8 +250,127 @@
     )(place, prob, d_out, qkv)
 
 
+EXTRA = 8
+OWNER_ROWS = 64
+
+
+def as_column(row, first, count):
+    size = row.shape[1]
+    here = lax.broadcasted_iota(jnp.int32, (count, size), 1) == first + lax.broadcasted_iota(
+        jnp.int32, (count, size), 0
+    )
+    return jnp.sum(jnp.where(here, row, 0.0), axis=1, keepdims=True)
+
+
+def blocks_kernel(seqs, members, q_ref, k_ref, v_ref, o_ref, gain_ref, table_ref, sent_ref):
+    shard = q_ref.shape[0]
+    width = q_ref.shape[1] // members
+    gain = as_column(gain_ref[...].astype(LOW).astype(F32), 0, shard)
+    parts = [
+        (ref[...].astype(LOW).astype(F32) * gain).astype(LOW) for ref in (q_ref, k_ref, v_ref)
+    ]
+    parts.append(o_ref[...].T.astype(LOW))
+    rest = jnp.zeros((EXTRA, sent_ref.shape[2]), LOW)
+    table_rows, heads = table_ref.shape
+    for seq in range(seqs):
+        for member in range(members):
+            at = seq * members + member
+            for i, part in enumerate(parts):
+                sent_ref[at, :shard, i * width : (i + 1) * width] = part[
+                    :, member * width : (member + 1) * width
+                ]
+            sent_ref[at, shard:, :] = rest
+            sent_ref[at, shard : shard + table_rows, :heads] = table_ref[...].astype(LOW)
+
+
+def attention_blocks(weights, w_out, gain, table, seqs, members):
+    shard, columns = weights[0].shape
+    return pl.pallas_call(
+        functools.partial(blocks_kernel, seqs, members),
+        out_shape=jax.ShapeDtypeStruct(
+            (seqs * members, shard + EXTRA, 4 * columns // members), LOW
+        ),
+        compiler_params=pltpu.CompilerParams(vmem_limit_bytes=32 * 2**20),
+        cost_estimate=pl.CostEstimate(
+            flops=0, bytes_accessed=16 * shard * columns, transcendentals=0
+        ),
+        name="attention_blocks",
+    )(*weights, w_out, gain, table)
+
+
+def owner_kernel(count, members, table_shape, *refs):
+    got_ref, extra_ref = refs[:2]
+    weight_refs = refs[2 : 2 + count]
+    gain_ref = refs[2 + count]
+    grad_refs = refs[3 + count : 3 + 2 * count]
+    sum_ref = refs[3 + 2 * count]
+    step = pl.program_id(0)
+    rows = got_ref.shape[1]
+    seqs = got_ref.shape[0] // members
+    width = got_ref.shape[2] // count
+    size = sum_ref.shape[1]
+    gain = as_column(gain_ref[...].astype(LOW).astype(F32), step * rows, rows)
+    total = jnp.zeros((rows, 1), F32)
+    for member in range(members):
+        product = sum(got_ref[seq * members + member].astype(F32) for seq in range(seqs))
+        for i in range(count):
+            part = product[:, i * width : (i + 1) * width]
+            here = pl.ds(member * width, width)
+            grad_refs[i][:, here] = part * gain
+            weight = weight_refs[i][:, here].astype(LOW).astype(F32)
+            total = total + jnp.sum(weight * part, axis=1, keepdims=True)
+
+    @pl.when(step == 0)
+    def _():
+        sum_ref[...] = jnp.zeros_like(sum_ref)
+
+    diagonal = lax.broadcasted_iota(jnp.int32, (rows, size), 1) == step * rows + (
+        lax.broadcasted_iota(jnp.int32, (rows, size), 0)
+    )
+    sum_ref[...] += jnp.sum(jnp.where(diagonal, total, 0.0), axis=0, keepdims=True)
+    if table_shape is not None:
+        table_rows, heads = table_shape
+        each = heads // members
+        for member in range(members):
+            piece = sum(extra_ref[seq * members + member].astype(F32) for seq in range(seqs))
+            refs[-1][:, member * each : (member + 1) * each] = piece[:table_rows, :each]
+
+
+def owner_grads(got, weights, gain, members, table_shape):
+    sources, height, columns = got.shape
+    shard, wide = weights[0].shape
+    count = len(weights)
+    rows = min(OWNER_ROWS, shard)
+    step_rows = pl.BlockSpec((rows, wide), lambda i: (i, 0))
+    row = pl.BlockSpec((1, shard), lambda i: (0, 0))
+    last = height // EXTRA - 1
+    out_specs = [step_rows] * count + [row]
+    out_shape = [jax.ShapeDtypeStruct((shard, wide), F32)] * count
+    out_shape.append(jax.ShapeDtypeStruct((1, shard), F32))
+    if table_shape is not None:
+        out_specs.append(pl.BlockSpec(table_shape, lambda i: (0, 0)))
+        out_shape.append(jax.ShapeDtypeStruct(table_shape, F32))
+    outs = pl.pallas_call(
+        functools.partial(owner_kernel, count, members, table_shape),
+        grid=(shard // rows,),
+        in_specs=[
+            pl.BlockSpec((sources, rows, columns), lambda i: (0, i, 0)),
+            pl.BlockSpec((sources, EXTRA, columns), lambda i: (0, last, 0)),
+        ]
+        + [step_rows] * count
+        + [row],
+        out_specs=out_specs,
+        out_shape=out_shape,
+        compiler_params=pltpu.CompilerParams(vmem_limit_bytes=32 * 2**20),
+        cost_estimate=pl.CostEstimate(
+            flops=0, bytes_accessed=10 * count * shard * wide, transcendentals=0
+        ),
+        name="owner_grads",
+    )(got, got, *weights, gain)
+    return outs[:count], outs[count], outs[-1] if table_shape is not None else None
+
+
 COLUMN = ("seq", "near", "core")
-EXTRA = 8
 
 
 def exchange(blocks, axes):
@@ -322,7 +445,7 @@
     mp_at = lax.axis_index("mp")
     member_at = near_at * CORES + core_at
     length = lax.dynamic_slice_in_dim(lengths, lax.axis_index("seq"), 1, 0)
-    place = jnp.concatenate([length, jnp.reshape(core_at, (1,)).astype(jnp.int32)])
+    place = jnp.stack([length[0], core_at.astype(jnp.int32), member_at.astype(jnp.int32)])
 
     def for_column(parts):
         return jnp.broadcast_to(parts[None], (seqs,) + parts.shape).reshape(
@@ -404,23 +527,8 @@
     def here(pair):
         return lax.dynamic_index_in_dim(pair, near_at, 0, keepdims=False)
 
-    attn_parts = jnp.moveaxis(
-        jnp.concatenate(
-            [
-                by_member(scaled(w_query, attn_scale)),
-                by_member(scaled(w_key, attn_scale)),
-                by_member(scaled(w_value, attn_scale)),
-                by_member(w_out.T.astype(LOW)),
-            ],
-            2,
-        ),
-        1,
-        0,
-    )
-    table_parts = rel_table.astype(LOW).reshape(table_rows, members, heads)
-    table_parts = jnp.moveaxis(table_parts, 1, 0).reshape(members, 1, table_rows * heads)
-    table_parts = jnp.pad(
-        table_parts, ((0, 0), (0, EXTRA - 1), (0, 4 * width - table_rows * heads))
+    attn_sent = attention_blocks(
+        (w_query, w_key, w_value), w_out, attn_scale.reshape(1, shard), rel_table, seqs, members
     )
     gate_up_parts = for_column(
         jnp.moveaxis(
@@ -433,20 +541,18 @@
     )
     down_parts = for_column(w_down.astype(LOW).reshape(members, hidden_width, shard))
 
-    attn_got = exchange(for_column(jnp.concatenate([attn_parts, table_parts], 1)), COLUMN)
+    attn_got = exchange(attn_sent, COLUMN)
     attn_weights = attn_got[:, :shard].reshape(model, 4 * width)
     qkv_weight = attn_weights[:, : 3 * width]
     out_weight_t = attn_weights[:, 3 * width :]
-    table = attn_got[:, shard, : table_rows * heads].reshape(buckets, heads)
-    table = jnp.pad(table.T, ((0, 8 - heads), (0, 0)))
+    table = attn_got[:, shard : shard + table_rows, :heads_mp].reshape(buckets, heads_mp)
 
     mine_inputs = near_block_rows(inputs)
     mine_values = mine_inputs.astype(F32)
     mine_normed = (mine_values * rms(mine_values)).astype(LOW)
     normed_rows = jnp.concatenate([mine_normed, swap(mine_normed, "core")], 0)
     row_valid = (member_at * tok_rows + lax.iota(jnp.int32, tok_rows) < length)[:, None]
-    later_cotangent = after(cotangent, mine_inputs)
-    masked = jnp.where(row_valid, later_cotangent, jnp.zeros_like(cotangent))
+    masked = jnp.where(row_valid, cotangent, jnp.zeros_like(cotangent))
     mine_grad = near_block_rows(masked)
     other_grad = swap(mine_grad, "core")
 
@@ -494,25 +600,17 @@
         )
         d_norms.append(contract_cols(d_gate_ups[-1], gate_up_weight))
     inner_cores = sum_cores(*d_norms)
-    ffn_cores = sum_cores(*[rows_dot(after(act, *inner_cores), down_weight) for act in acts])
     d_gate_ups = [after(grad, *d_norms) for grad in d_gate_ups]
 
     def to_owners(grad):
         return exchange(grad, COLUMN)
-
-    def of_owner(got):
-        parts = got.reshape((seqs, members) + got.shape[1:]).astype(F32)
-        return jnp.moveaxis(jnp.sum(parts, axis=0), 0, 1)
-
-    def flat(parts):
-        return parts.reshape(shard, -1)
 
     def by_rows(got):
         parts = got.reshape((seqs, members) + got.shape[1:]).astype(F32)
         return jnp.sum(parts, axis=0).reshape(-1, shard)
 
     d_down = to_owners(jnp.moveaxis(d_down_w.reshape(hidden_width, sources, shard), 1, 0))
-    inner_two, inner_moved = sum_near_both(after(sum_mp(inner_cores), d_down, *ffn_cores))
+    inner_two, inner_moved = sum_near_both(after(sum_mp(inner_cores), d_down))
     d_gate_up_w = (
         contract_rows(halves[0], d_gate_ups[0]) + contract_rows(halves[1], d_gate_ups[1])
     ).astype(LOW)
@@ -526,6 +624,7 @@
     pair_valid = pair_first < length
     grad_one = pair_cotangent + norm_grad(inner_two, normed_two, inv_two)
     mine_one, other_one = gather_rows(grad_one.astype(LOW))
+    ffn_cores = sum_cores(*[rows_dot(after(act, inner_moved), down_weight) for act in acts])
     d_attended = jnp.concatenate(
         [rows_dot(mine_one, out_weight_t), rows_dot(other_one, out_weight_t)], 0
     ).astype(LOW)
@@ -535,13 +634,15 @@
     )
     ffn_moved, ffn_kept = send_mp([after(rows, mine_one) for rows in ffn_cores])
     ffn_moved = [after(rows, d_qkv) for rows in ffn_moved]
-    inner_one = sum_near(after(sum_mp(inner_cores), d_gate_up))
-    table_sent = d_table[:, :heads].astype(LOW).reshape(sources, 1, table_rows * heads)
+    last_moved, last_kept = send_mp(inner_cores)
+    inner_one = sum_near(sum((piece.astype(F32) for piece in last_moved), last_kept))
+    table_sent = d_table[:, :heads].astype(LOW).reshape(sources, table_rows, heads)
     table_sent = jnp.pad(
-        table_sent, ((0, 0), (0, EXTRA - 1), (0, 3 * width - table_rows * heads))
+        table_sent, ((0, 0), (0, EXTRA - table_rows), (0, 3 * width - heads))
     )
     d_qkv_w = contract_rows(normed_rows, d_qkv).astype(LOW).reshape(sources, shard, -1)
-    d_qkv_got = to_owners(after(jnp.concatenate([d_qkv_w, table_sent], 1), d_gate_up))
+    d_qkv_sent = jnp.concatenate([d_qkv_w, table_sent], 1)
+    d_qkv_got = to_owners(after(d_qkv_sent, d_gate_up, last_moved[0]))
     later_attended = after(attended, inner_cores[0])
     d_out = contract_rows(later_attended[:half_rows], mine_one) + contract_rows(
         later_attended[half_rows:], other_one
@@ -556,41 +657,32 @@
     ffn_pair = sum((piece.astype(F32) for piece in ffn_moved), ffn_kept)
     after_ffn = here(after_attn) + sum_near(after(ffn_pair, inner_one))
     own_out = jnp.where(here(pair_valid), after_ffn, 0.0).astype(LOW)
-    layer_out = over_mp(own_out, 0).reshape(tok_rows, model)
-
-    g_gate_up = of_owner(after(d_gate_up, inner_cores[0]))
-    g_gate, g_up = flat(g_gate_up[:, :, :hidden_width]), flat(g_gate_up[:, :, hidden_width:])
-    got_qkv = of_owner(d_qkv_got)
-    g_query, g_key, g_value = (
-        flat(got_qkv[:shard, :, i * width : (i + 1) * width]) for i in range(3)
-    )
-    d_rel_table = got_qkv[shard, :, : table_rows * heads].reshape(members, table_rows, heads)
-    d_rel_table = jnp.moveaxis(d_rel_table, 0, 1).reshape(table_rows, heads_mp)
-
-    def gain_grad(pairs):
-        return sum(jnp.sum(w.astype(LOW).astype(F32) * g, axis=1) for w, g in pairs)
-
-    gains = jnp.stack(
-        [
-            gain_grad([(w_query, g_query), (w_key, g_key), (w_value, g_value)]),
-            gain_grad([(w_gate, g_gate), (w_up, g_up)]),
-        ]
-    )
+    layer_out = over_mp(after(own_out, d_qkv_got), 0).reshape(tok_rows, model)
+
+    (d_w_gate, d_w_up), ffn_gain, _ = owner_grads(
+        after(d_gate_up, inner_cores[0]), (w_gate, w_up), ffn_scale.reshape(1, shard), members, None
+    )
+    (d_w_query, d_w_key, d_w_value), attn_gain, d_rel_table = owner_grads(
+        d_qkv_got,
+        (w_query, w_key, w_value),
+        attn_scale.reshape(1, shard),
+        members,
+        (table_rows, heads_mp),
+    )
+    gains = jnp.concatenate([attn_gain, ffn_gain], 0)
     gains = sum((shifted(gains, away) for away in range(1, mp_count)), gains)
-    attn_gain = attn_scale.astype(LOW).astype(F32)[:, None]
-    ffn_gain = ffn_scale.astype(LOW).astype(F32)[:, None]
     return (
         layer_out,
         d_inputs,
         gains[0],
-        g_query * attn_gain,
-        g_key * attn_gain,
-        g_value * attn_gain,
+        d_w_query,
+        d_w_key,
+        d_w_value,
         by_rows(d_out),
         d_rel_table,
         gains[1],
-        g_gate * ffn_gain,
-        g_up * ffn_gain,
+        d_w_gate,
+        d_w_up,
         by_rows(after(d_down, d_qkv)),
     )
 

time: 533 us -> 477 us (0.89)
  local copies, waits for them, and re-layouts: 82.2 us -> 50.5 us
  waiting for transfers between devices: 209 us -> 195 us
  other arithmetic: 55.3 us -> 41.6 us
  Pallas kernels: 20 us -> 30.6 us
  matrix products: 66.4 us -> 59.6 us
    unnamed x130 -> x107, local copies, waits for them, and re-layouts: 29 us -> 11.4 us
    slice x11 -> x2, local copies, waits for them, and re-layouts: 13.2 us -> 0.75 us  [the longest x1 0.75 us: local(): attn_got[:, shard:shard + table_rows, :heads_mp].reshape(buckets, heads_mp)]
    ppermute x32, waiting for transfers between devices: 56.6 us -> 44.1 us  [swap(): return lax.ppermute(block, axis, [(0, 1), (1, 0)])]
    pallas_call x0 -> x3, Pallas kernels: none -> 10.5 us  [the longest x2 8.67 us: owner_grads(): pl.pallas_call(functools.partial(owner_kernel, count, members, table_shap...]
    ppermute x33, waiting for transfers between devices: 126 us -> 119 us  [shifted(): return lax.ppermute(block, 'mp', [(i, i ^ away) for i in range(mp_count)])]
    dot_general x8, matrix products: 29 us -> 22.7 us  [contract_cols(): lax.dot_general(left, right, (((1,), (1,)), ((), ())), preferred_element_...]
    all_to_all x7, waiting for transfers between devices: 25.6 us -> 31.7 us  [exchange(): return lax.all_to_all(blocks, axes, split_axis=0, concat_axis=0, tiled=True)]
    mul x2 -> x0, other arithmetic: 5.93 us -> none  [the longest x1 3.56 us: local(): g_up * ffn_gain]
  transfers between devices with their start and end apart: 72 -> 72, of which waited for: 28 -> 35; matrix products, arithmetic and copies ran while one was open for 30% -> 22% of each run, Pallas kernels for 4% -> 6%
where the time goes in v1:
time: 477 us; the launch traced here: 468 us
  waiting for transfers between devices  195 us (41%)
  starting transfers between devices  88.5 us (19%)
  matrix products  59.6 us (12%)
  local copies, waits for them, and re-layouts  50.5 us (11%)
  other arithmetic  41.6 us (9%)
  Pallas kernels  30.6 us (6%)
    ppermute x33, waiting for transfers between devices, shifted(): return lax.ppermute(block, 'mp', [(i, i ^ away) for i in range(mp_count)])  119 us
    ppermute x32, waiting for transfers between devices, swap(): return lax.ppermute(block, axis, [(0, 1), (1, 0)])  44.1 us
    ppermute x33, starting transfers between devices, shifted(): return lax.ppermute(block, 'mp', [(i, i ^ away) for i in range(mp_count)])  40.2 us
    all_to_all x7, starting transfers between devices, exchange(): return lax.all_to_all(blocks, axes, split_axis=0, concat_axis=0, tiled=True)  32.8 us
    all_to_all x7, waiting for transfers between devices, exchange(): return lax.all_to_all(blocks, axes, split_axis=0, concat_axis=0, tiled=True)  31.7 us
    dot_general x8, matrix products, contract_cols(): lax.dot_general(left, right, (((1,), (1,)), ((), ())), preferred_element_...  22.7 us
    dot_general x7, matrix products, contract_rows(): lax.dot_general(left, right, (((0,), (0,)), ((), ())), preferred_element_...  20.9 us
    dot_general x7, matrix products, rows_dot(): return jnp.dot(left, right, preferred_element_type=F32)  16 us
  transfers between devices with their start and end apart: 72, of which 35 were waited for; matrix products, arithmetic and copies ran while one was open for 22% of the time, Pallas kernels for 6%

profile of v1, /device:TPU:0, one launch (start us, length us, event | category | flops | bytes accessed | tf_op | source)
XLA Modules:
  0.0 468.2 jit_solution(9874531062346523849)
XLA Ops:
  10.5 5.3 %all-to-all-start = ((bf16[8,264,512]{2,1,0:T(8,128)(2,1)}), bf16[8,264,512]{2,1,0:T(8,128)(2,1)}, u32[]{:S(2)}, u32[]{:S(2)}) async-start(bf16[8,264,512]{2,1,0:T(8,128)(2,1)} %attention_blocks.1), calls=%async_computation | async-start | bytes 4325376 | tf_op jit(solution)/shard_map/all_to_all | solution.py:377
  36.8 5.5 %collective-permute-done.2 = bf16[64,2048]{1,0:T(8,128)(2,1)S(1)} collective-permute-done((bf16[64,2048]{1,0:T(8,128)(2,1)}, bf16[64,2048]{1,0:T(8,128)(2,1)S(1)}, u32[]{:S(2)}, u32[]{:S(2)}) %collective-permute-start.2) | collective-permute-done | bytes 262176 | tf_op jit(solution)/shard_map/ppermute | solution.py:471
  53.8 4.9 %pad_maximum_fusion = bf16[1024,2048]{1,0:T(8,128)(2,1)} fusion(bf16[512,2048]{1,0:T(8,128)(2,1)} %collective-permute-done.4, bf16[512,2048]{1,0:T(8,128)(2,1)} %multiply_convert_fusion), kind=kLoop, calls=%fused_computation.1 | loop fusion | flops 8388608 | bytes 8388608 | tf_op jit(solution)/shard_map/concatenate | solution.py:553
  71.6 7.5 %attention_forward.1 = (bf16[1024,128]{1,0:T(8,128)(2,1)S(1)}, bf16[2,1024,1024]{2,1,0:T(8,128)(2,1)S(1)}) custom-call(s32[3]{0:T(128)S(1)} %pad_add_fusion.place_ref, bf16[1024,384]{1,0:T(8,128)(2,1)S(1)} %convolution_convert_fusion.4.qkv_ref, bf16[32,8]{1,0:T(8,128)(2,1)S(1)} %bitcast.346), custom_call_target="tpu_custom_call" | custom-call | flops 536870912 | bytes 4194304 | tf_op jit(solution)/shard_map/attention_forward/pallas_call | solution.py:121
  96.6 12.2 %collective-permute-done.12 = bf16[2,64,2048]{2,1,0:T(8,128)(2,1)S(1)} collective-permute-done((bf16[2,64,2048]{2,1,0:T(8,128)(2,1)S(1)}, bf16[2,64,2048]{2,1,0:T(8,128)(2,1)S(1)}, u32[]{:S(2)}, u32[]{:S(2)}) %collective-permute-start.12) | collective-permute-done | bytes 524320 | tf_op jit(solution)/shard_map/ppermute | solution.py:471
  108.8 10.6 %collective-permute-done.14 = bf16[2,64,2048]{2,1,0:T(8,128)(2,1)S(1)} collective-permute-done((bf16[2,64,2048]{2,1,0:T(8,128)(2,1)S(1)}, bf16[2,64,2048]{2,1,0:T(8,128)(2,1)S(1)}, u32[]{:S(2)}, u32[]{:S(2)}) %collective-permute-start.14) | collective-permute-done | bytes 524320 | tf_op jit(solution)/shard_map/ppermute | solution.py:471
  121.7 12.2 %collective-permute-done.17 = bf16[2,64,2048]{2,1,0:T(8,128)(2,1)} collective-permute-done((bf16[2,64,2048]{2,1,0:T(8,128)(2,1)S(1)}, bf16[2,64,2048]{2,1,0:T(8,128)(2,1)}, u32[]{:S(2)}, u32[]{:S(2)}) %collective-permute-start.17) | collective-permute-done | bytes 524320 | tf_op jit(solution)/shard_map/ppermute | solution.py:381
  153.0 5.2 %collective-permute-done.18 = bf16[2,64,2048]{2,1,0:T(8,128)(2,1)} collective-permute-done((bf16[2,64,2048]{2,1,0:T(8,128)(2,1)}, bf16[2,64,2048]{2,1,0:T(8,128)(2,1)}, u32[]{:S(2)}, u32[]{:S(2)}) %collective-permute-start.18) | collective-permute-done | bytes 524320 | tf_op jit(solution)/shard_map/ppermute | solution.py:471
  160.1 12.5 %collective-permute-done.19 = bf16[2,64,2048]{2,1,0:T(8,128)(2,1)S(1)} collective-permute-done((bf16[2,64,2048]{2,1,0:T(8,128)(2,1)}, bf16[2,64,2048]{2,1,0:T(8,128)(2,1)S(1)}, u32[]{:S(2)}, u32[]{:S(2)}) %collective-permute-start.19) | collective-permute-done | bytes 524320 | tf_op jit(solution)/shard_map/ppermute | solution.py:471
  179.8 19.2 %all-to-all-done.2 = bf16[8,256,640]{2,1,0:T(8,128)(2,1)} async-done(((bf16[8,256,640]{2,1,0:T(8,128)(2,1)}), bf16[8,256,640]{2,1,0:T(8,128)(2,1)}, u32[]{:S(2)}, u32[]{:S(2)}) %all-to-all-start.2) | async-done | bytes 2621472 | tf_op jit(solution)/shard_map/all_to_all | solution.py:377
  221.0 5.2 %fusion.69 = bf16[512,2048]{1,0:T(8,128)(2,1)} fusion(bf16[512,640]{1,0:T(8,128)(2,1)S(1)} %pad_maximum_fusion.4, bf16[2048,640]{1,0:T(8,128)(2,1)} %bitcast.51), kind=kOutput, calls=%fused_computation.207 | convolution fusion | flops 1342177280 | bytes 5373952 | tf_op jit(solution)/shard_map/dot_general | solution.py:393
  250.6 5.8 %fusion.70 = f32[2048,640]{1,0:T(8,128)} fusion(bf16[512,2048]{1,0:T(8,128)(2,1)} %bitcast.50, bf16[512,640]{1,0:T(8,128)(2,1)S(1)} %copy-done.41), kind=kOutput, calls=%fused_computation.208 | convolution fusion | flops 1342177280 | bytes 7995392 | tf_op jit(solution)/shard_map/dot_general | solution.py:397
  257.9 10.7 %collective-permute-done.29 = bf16[2,64,2048]{2,1,0:T(8,128)(2,1)} collective-permute-done((bf16[2,64,2048]{2,1,0:T(8,128)(2,1)}, bf16[2,64,2048]{2,1,0:T(8,128)(2,1)}, u32[]{:S(2)}, u32[]{:S(2)}) %collective-permute-start.29) | collective-permute-done | bytes 524320 | tf_op jit(solution)/shard_map/ppermute | solution.py:471
  273.5 6.5 %add_convert_fusion = bf16[2048,640]{1,0:T(8,128)(2,1)} fusion(f32[2048,640]{1,0:T(8,128)} %fusion.70, bf16[512,2048]{1,0:T(8,128)(2,1)} %bitcast.60, bf16[512,640]{1,0:T(8,128)(2,1)S(1)} %copy-done.39), kind=kOutput, calls=%fused_computation | convolution fusion | flops 1344798720 | bytes 10616832 | tf_op jit(solution)/shard_map/dot_general | solution.py:397
  279.9 5.8 %collective-permute-done.32 = bf16[2,64,2048]{2,1,0:T(8,128)(2,1)S(1)} collective-permute-done((bf16[2,64,2048]{2,1,0:T(8,128)(2,1)}, bf16[2,64,2048]{2,1,0:T(8,128)(2,1)S(1)}, u32[]{:S(2)}, u32[]{:S(2)}) %collective-permute-start.32) | collective-permute-done | bytes 524320 | tf_op jit(solution)/shard_map/ppermute | solution.py:381
  293.1 5.0 %all-to-all-start.4 = ((bf16[8,256,640]{2,1,0:T(8,128)(2,1)}), bf16[8,256,640]{2,1,0:T(8,128)(2,1)S(1)}, u32[]{:S(2)}, u32[]{:S(2)}) async-start(bf16[8,256,640]{2,1,0:T(8,128)(2,1)} %bitcast.350), calls=%async_computation.4 | async-start | bytes 5242880 | tf_op jit(solution)/shard_map/all_to_all | solution.py:377
  310.5 12.2 %collective-permute-done.36 = bf16[2,64,2048]{2,1,0:T(8,128)(2,1)S(1)} collective-permute-done((bf16[2,64,2048]{2,1,0:T(8,128)(2,1)}, bf16[2,64,2048]{2,1,0:T(8,128)(2,1)S(1)}, u32[]{:S(2)}, u32[]{:S(2)}) %collective-permute-start.36) | collective-permute-done | bytes 524320 | tf_op jit(solution)/shard_map/ppermute | solution.py:471
  331.7 12.5 %attention_backward.1 = (bf16[1024,384]{1,0:T(8,128)(2,1)S(1)}, f32[32,128]{1,0:T(8,128)S(1)}) custom-call(s32[3]{0:T(128)S(1)} %pad_add_fusion.place_ref, bf16[2,1024,1024]{2,1,0:T(8,128)(2,1)S(1)} %copy-done.14, bf16[1024,128]{1,0:T(8,128)(2,1)S(1)} %pad_maximum_fusion.5.do_ref, bf16[1024,384]{1,0:T(8,128)(2,1)S(1)} %copy-done.16), custom_call_target="tpu_custom_call" | custom-call | flops 4294967296 | bytes 4194304 | tf_op jit(solution)/shard_map/attention_backward/pallas_call | solution.py:221
  362.9 7.3 %collective-permute-done.49 = bf16[2,64,2048]{2,1,0:T(8,128)(2,1)S(1)} collective-permute-done((bf16[2,64,2048]{2,1,0:T(8,128)(2,1)S(1)}, bf16[2,64,2048]{2,1,0:T(8,128)(2,1)S(1)}, u32[]{:S(2)}, u32[]{:S(2)}) %collective-permute-start.49) | collective-permute-done | bytes 524320 | tf_op jit(solution)/shard_map/ppermute | solution.py:471
  370.2 10.8 %collective-permute-done.51 = bf16[2,64,2048]{2,1,0:T(8,128)(2,1)S(1)} collective-permute-done((bf16[2,64,2048]{2,1,0:T(8,128)(2,1)S(1)}, bf16[2,64,2048]{2,1,0:T(8,128)(2,1)S(1)}, u32[]{:S(2)}, u32[]{:S(2)}) %collective-permute-start.51) | collective-permute-done | bytes 524320 | tf_op jit(solution)/shard_map/ppermute | solution.py:471
  384.5 5.3 %collective-permute-done.54 = bf16[64,2048]{1,0:T(8,128)(2,1)S(1)} collective-permute-done((bf16[64,2048]{1,0:T(8,128)(2,1)S(1)}, bf16[64,2048]{1,0:T(8,128)(2,1)S(1)}, u32[]{:S(2)}, u32[]{:S(2)}) %collective-permute-start.54) | collective-permute-done | bytes 262176 | tf_op jit(solution)/shard_map/ppermute | solution.py:381
  407.5 5.2 %collective-permute-done.60 = bf16[64,2048]{1,0:T(8,128)(2,1)S(1)} collective-permute-done((bf16[64,2048]{1,0:T(8,128)(2,1)S(1)}, bf16[64,2048]{1,0:T(8,128)(2,1)S(1)}, u32[]{:S(2)}, u32[]{:S(2)}) %collective-permute-start.60) | collective-permute-done | bytes 262176 | tf_op jit(solution)/shard_map/ppermute | solution.py:471
  412.8 15.6 %collective-permute-done.55 = bf16[64,2048]{1,0:T(8,128)(2,1)S(1)} collective-permute-done((bf16[64,2048]{1,0:T(8,128)(2,1)S(1)}, bf16[64,2048]{1,0:T(8,128)(2,1)S(1)}, u32[]{:S(2)}, u32[]{:S(2)}) %collective-permute-start.55) | collective-permute-done | bytes 262176 | tf_op jit(solution)/shard_map/ppermute | solution.py:381
  460.5 6.4 %all-to-all-done.6 = bf16[8,128,256]{2,1,0:T(8,128)(2,1)S(1)} async-done(((bf16[8,128,256]{2,1,0:T(8,128)(2,1)}), bf16[8,128,256]{2,1,0:T(8,128)(2,1)S(1)}, u32[]{:S(2)}, u32[]{:S(2)}) %all-to-all-start.6) | async-done | bytes 524320 | tf_op jit(solution)/shard_map/all_to_all | solution.py:377
  (362 shorter events, 256.6 us)
Async XLA Ops:
  10.5 55.9 %all-to-all-start = ((bf16[8,264,512]{2,1,0:T(8,128)(2,1)}), bf16[8,264,512]{2,1,0:T(8,128)(2,1)}, u32[]{:S(2)}, u32[]{:S(2)}) async-start(bf16[8,264,512]{2,1,0:T(8,128)(2,1)} %attention_blocks.1), calls=%async_computation | async-start | bytes 4325376 | tf_op jit(solution)/shard_map/all_to_all | solution.py:377
  48.0 33.2 %collective-permute-start.9 = (bf16[512,2048]{1,0:T(8,128)(2,1)}, bf16[512,2048]{1,0:T(8,128)(2,1)}, u32[]{:S(2)}, u32[]{:S(2)}) collective-permute-start(bf16[512,2048]{1,0:T(8,128)(2,1)} %bitcast.30), channel_id=1, source_target_pairs={{0,4},{4,0},{1,5},{5,1},{2,6},{6,2},{3,7},{7,3},{8,12},{12,8},{9,1... | collective-permute-start | bytes 6291464 | tf_op jit(solution)/shard_map/ppermute | solution.py:381
  83.2 36.7 %all-to-all-start.1 = ((bf16[8,320,256]{2,1,0:T(8,128)(2,1)}), bf16[8,320,256]{2,1,0:T(8,128)(2,1)S(1)}, u32[]{:S(2)}, u32[]{:S(2)}) async-start(bf16[8,320,256]{2,1,0:T(8,128)(2,1)} %bitcast.15), calls=%async_computation.1 | async-start | bytes 2621440 | tf_op jit(solution)/shard_map/all_to_all | solution.py:377
  95.5 23.9 %collective-permute-start.14 = (bf16[2,64,2048]{2,1,0:T(8,128)(2,1)S(1)}, bf16[2,64,2048]{2,1,0:T(8,128)(2,1)S(1)}, u32[]{:S(2)}, u32[]{:S(2)}) collective-permute-start(bf16[2,64,2048]{2,1,0:T(8,128)(2,1)S(1)} %get-tuple-element.113), channel_id=1, source_target_pairs={{0,2},{1,3},{2,0},{3,1},{4,6},{5,7},{6,4},{7,5},{8,10},{9,11},{10,... | collective-permute-start | bytes 1572872 | tf_op jit(solution)/shard_map/ppermute | solution.py:471
  96.0 23.5 %collective-permute-start.16 = (bf16[2,64,2048]{2,1,0:T(8,128)(2,1)S(1)}, bf16[2,64,2048]{2,1,0:T(8,128)(2,1)S(1)}, u32[]{:S(2)}, u32[]{:S(2)}) collective-permute-start(bf16[2,64,2048]{2,1,0:T(8,128)(2,1)S(1)} %get-tuple-element.112), channel_id=1, source_target_pairs={{0,1},{1,0},{2,3},{3,2},{4,5},{5,4},{6,7},{7,6},{8,9},{9,8},{10,11... | collective-permute-start | bytes 1572872 | tf_op jit(solution)/shard_map/ppermute | solution.py:471
  133.9 65.2 %all-to-all-start.2 = ((bf16[8,256,640]{2,1,0:T(8,128)(2,1)}), bf16[8,256,640]{2,1,0:T(8,128)(2,1)}, u32[]{:S(2)}, u32[]{:S(2)}) async-start(bf16[8,256,640]{2,1,0:T(8,128)(2,1)} %bitcast.367), calls=%async_computation.2 | async-start | bytes 5242880 | tf_op jit(solution)/shard_map/all_to_all | solution.py:377
  147.1 25.5 %collective-permute-start.19 = (bf16[2,64,2048]{2,1,0:T(8,128)(2,1)}, bf16[2,64,2048]{2,1,0:T(8,128)(2,1)S(1)}, u32[]{:S(2)}, u32[]{:S(2)}) collective-permute-start(bf16[2,64,2048]{2,1,0:T(8,128)(2,1)} %get-tuple-element.100), channel_id=1, source_target_pairs={{0,2},{1,3},{2,0},{3,1},{4,6},{5,7},{6,4},{7,5},{8,10},{9,11},{10,... | collective-permute-start | bytes 1572872 | tf_op jit(solution)/shard_map/ppermute | solution.py:471
  151.3 22.1 %collective-permute-start.20 = (bf16[2,64,2048]{2,1,0:T(8,128)(2,1)}, bf16[2,64,2048]{2,1,0:T(8,128)(2,1)S(1)}, u32[]{:S(2)}, u32[]{:S(2)}) collective-permute-start(bf16[2,64,2048]{2,1,0:T(8,128)(2,1)} %get-tuple-element.100), channel_id=1, source_target_pairs={{0,3},{1,2},{2,1},{3,0},{4,7},{5,6},{6,5},{7,4},{8,11},{9,10},{10,... | collective-permute-start | bytes 1572872 | tf_op jit(solution)/shard_map/ppermute | solution.py:471
  153.0 21.8 %collective-permute-start.21 = (bf16[2,64,2048]{2,1,0:T(8,128)(2,1)}, bf16[2,64,2048]{2,1,0:T(8,128)(2,1)S(1)}, u32[]{:S(2)}, u32[]{:S(2)}) collective-permute-start(bf16[2,64,2048]{2,1,0:T(8,128)(2,1)} %get-tuple-element.100), channel_id=1, source_target_pairs={{0,4},{4,0},{1,5},{5,1},{2,6},{6,2},{3,7},{7,3},{8,12},{12,8},{9,1... | collective-permute-start | bytes 1572872 | tf_op jit(solution)/shard_map/ppermute | solution.py:381
  158.2 19.0 %collective-permute-start.22 = (bf16[2,64,2048]{2,1,0:T(8,128)(2,1)}, bf16[2,64,2048]{2,1,0:T(8,128)(2,1)S(1)}, u32[]{:S(2)}, u32[]{:S(2)}) collective-permute-start(bf16[2,64,2048]{2,1,0:T(8,128)(2,1)} %collective-permute-done.18), channel_id=1, source_target_pairs={{0,4},{4,0},{1,5},{5,1},{2,6},{6,2},{3,7},{7,3},{8,12},{12,8},{9,1... | collective-permute-start | bytes 1572872 | tf_op jit(solution)/shard_map/ppermute | solution.py:381
  227.3 44.5 %all-to-all-start.3 = ((bf16[8,320,256]{2,1,0:T(8,128)(2,1)}), bf16[8,320,256]{2,1,0:T(8,128)(2,1)}, u32[]{:S(2)}, u32[]{:S(2)}) async-start(bf16[8,320,256]{2,1,0:T(8,128)(2,1)} %bitcast.382), calls=%async_computation.3 | async-start | bytes 2621440 | tf_op jit(solution)/shard_map/all_to_all | solution.py:377
  235.3 21.0 %collective-permute-start.25 = (bf16[2,64,2048]{2,1,0:T(8,128)(2,1)}, bf16[2,64,2048]{2,1,0:T(8,128)(2,1)}, u32[]{:S(2)}, u32[]{:S(2)}) collective-permute-start(bf16[2,64,2048]{2,1,0:T(8,128)(2,1)} %get-tuple-element.122), channel_id=1, source_target_pairs={{0,4},{4,0},{1,5},{5,1},{2,6},{6,2},{3,7},{7,3},{8,12},{12,8},{9,1... | collective-permute-start | bytes 1572872 | tf_op jit(solution)/shard_map/ppermute | solution.py:381
  243.0 25.6 %collective-permute-start.29 = (bf16[2,64,2048]{2,1,0:T(8,128)(2,1)}, bf16[2,64,2048]{2,1,0:T(8,128)(2,1)}, u32[]{:S(2)}, u32[]{:S(2)}) collective-permute-start(bf16[2,64,2048]{2,1,0:T(8,128)(2,1)} %get-tuple-element.110), channel_id=1, source_target_pairs={{0,2},{1,3},{2,0},{3,1},{4,6},{5,7},{6,4},{7,5},{8,10},{9,11},{10,... | collective-permute-start | bytes 1572872 | tf_op jit(solution)/shard_map/ppermute | solution.py:471
  244.9 23.9 %collective-permute-start.31 = (bf16[2,64,2048]{2,1,0:T(8,128)(2,1)}, bf16[2,64,2048]{2,1,0:T(8,128)(2,1)}, u32[]{:S(2)}, u32[]{:S(2)}) collective-permute-start(bf16[2,64,2048]{2,1,0:T(8,128)(2,1)} %get-tuple-element.109), channel_id=1, source_target_pairs={{0,1},{1,0},{2,3},{3,2},{4,5},{5,4},{6,7},{7,6},{8,9},{9,8},{10,11... | collective-permute-start | bytes 1572872 | tf_op jit(solution)/shard_map/ppermute | solution.py:471
  291.4 35.8 %collective-permute-start.39 = (bf16[2,64,2048]{2,1,0:T(8,128)(2,1)}, bf16[2,64,2048]{2,1,0:T(8,128)(2,1)}, u32[]{:S(2)}, u32[]{:S(2)}) collective-permute-start(bf16[2,64,2048]{2,1,0:T(8,128)(2,1)} %get-tuple-element.97), channel_id=1, source_target_pairs={{0,4},{4,0},{1,5},{5,1},{2,6},{6,2},{3,7},{7,3},{8,12},{12,8},{9,1... | collective-permute-start | bytes 1572872 | tf_op jit(solution)/shard_map/ppermute | solution.py:381
  293.1 97.7 %all-to-all-start.4 = ((bf16[8,256,640]{2,1,0:T(8,128)(2,1)}), bf16[8,256,640]{2,1,0:T(8,128)(2,1)S(1)}, u32[]{:S(2)}, u32[]{:S(2)}) async-start(bf16[8,256,640]{2,1,0:T(8,128)(2,1)} %bitcast.350), calls=%async_computation.4 | async-start | bytes 5242880 | tf_op jit(solution)/shard_map/all_to_all | solution.py:377
  323.4 22.9 %collective-permute-start.38 = (bf16[2,64,2048]{2,1,0:T(8,128)(2,1)S(1)}, bf16[2,64,2048]{2,1,0:T(8,128)(2,1)S(1)}, u32[]{:S(2)}, u32[]{:S(2)}) collective-permute-start(bf16[2,64,2048]{2,1,0:T(8,128)(2,1)S(1)} %get-tuple-element.65), channel_id=1, source_target_pairs={{0,3},{1,2},{2,1},{3,0},{4,7},{5,6},{6,5},{7,4},{8,11},{9,10},{10,... | collective-permute-start | bytes 1572872 | tf_op jit(solution)/shard_map/ppermute | solution.py:471
  324.8 24.3 %collective-permute-start.44 = (bf16[2,64,2048]{2,1,0:T(8,128)(2,1)S(1)}, bf16[2,64,2048]{2,1,0:T(8,128)(2,1)S(1)}, u32[]{:S(2)}, u32[]{:S(2)}) collective-permute-start(bf16[2,64,2048]{2,1,0:T(8,128)(2,1)S(1)} %get-tuple-element.69), channel_id=1, source_target_pairs={{0,2},{1,3},{2,0},{3,1},{4,6},{5,7},{6,4},{7,5},{8,10},{9,11},{10,... | collective-permute-start | bytes 1572872 | tf_op jit(solution)/shard_map/ppermute | solution.py:471
  326.6 22.6 %collective-permute-start.46 = (bf16[2,64,2048]{2,1,0:T(8,128)(2,1)S(1)}, bf16[2,64,2048]{2,1,0:T(8,128)(2,1)S(1)}, u32[]{:S(2)}, u32[]{:S(2)}) collective-permute-start(bf16[2,64,2048]{2,1,0:T(8,128)(2,1)S(1)} %get-tuple-element.71), channel_id=1, source_target_pairs={{0,1},{1,0},{2,3},{3,2},{4,5},{5,4},{6,7},{7,6},{8,9},{9,8},{10,11... | collective-permute-start | bytes 1572872 | tf_op jit(solution)/shard_map/ppermute | solution.py:471
  356.3 24.7 %collective-permute-start.51 = (bf16[2,64,2048]{2,1,0:T(8,128)(2,1)S(1)}, bf16[2,64,2048]{2,1,0:T(8,128)(2,1)S(1)}, u32[]{:S(2)}, u32[]{:S(2)}) collective-permute-start(bf16[2,64,2048]{2,1,0:T(8,128)(2,1)S(1)} %get-tuple-element.103), channel_id=1, source_target_pairs={{0,2},{1,3},{2,0},{3,1},{4,6},{5,7},{6,4},{7,5},{8,10},{9,11},{10,... | collective-permute-start | bytes 1572872 | tf_op jit(solution)/shard_map/ppermute | solution.py:471
  357.8 23.2 %collective-permute-start.53 = (bf16[2,64,2048]{2,1,0:T(8,128)(2,1)S(1)}, bf16[2,64,2048]{2,1,0:T(8,128)(2,1)S(1)}, u32[]{:S(2)}, u32[]{:S(2)}) collective-permute-start(bf16[2,64,2048]{2,1,0:T(8,128)(2,1)S(1)} %get-tuple-element.104), channel_id=1, source_target_pairs={{0,1},{1,0},{2,3},{3,2},{4,5},{5,4},{6,7},{7,6},{8,9},{9,8},{10,11... | collective-permute-start | bytes 1572872 | tf_op jit(solution)/shard_map/ppermute | solution.py:471
  390.8 43.8 %all-to-all-start.5 = ((bf16[8,264,384]{2,1,0:T(8,128)(2,1)}), bf16[8,264,384]{2,1,0:T(8,128)(2,1)}, u32[]{:S(2)}, u32[]{:S(2)}) async-start(bf16[8,264,384]{2,1,0:T(8,128)(2,1)} %fusion.3), calls=%async_computation.5 | async-start | bytes 3244032 | tf_op jit(solution)/shard_map/all_to_all | solution.py:377
  401.0 27.4 %collective-permute-start.55 = (bf16[64,2048]{1,0:T(8,128)(2,1)S(1)}, bf16[64,2048]{1,0:T(8,128)(2,1)S(1)}, u32[]{:S(2)}, u32[]{:S(2)}) collective-permute-start(bf16[64,2048]{1,0:T(8,128)(2,1)S(1)} %fusion.56), channel_id=1, source_target_pairs={{0,8},{8,0},{1,9},{9,1},{2,10},{10,2},{3,11},{11,3},{4,12},{12,4},... | collective-permute-start | bytes 786440 | tf_op jit(solution)/shard_map/ppermute | solution.py:381
  447.0 19.9 %all-to-all-start.6 = ((bf16[8,128,256]{2,1,0:T(8,128)(2,1)}), bf16[8,128,256]{2,1,0:T(8,128)(2,1)S(1)}, u32[]{:S(2)}, u32[]{:S(2)}) async-start(bf16[8,128,256]{2,1,0:T(8,128)(2,1)} %bitcast.345), calls=%async_computation.6 | async-start | bytes 1048576 | tf_op jit(solution)/shard_map/all_to_all | solution.py:377
  (100 other events, 1006.4 us)

commit v2 on v1

--- a/solution.py
+++ b/solution.py
@@ -370,6 +370,221 @@
     return outs[:count], outs[count], outs[-1] if table_shape is not None else None
 
 
+def rows_dot(left, right):
+    return jnp.dot(left, right, preferred_element_type=F32)
+
+
+def contract_cols(left, right):
+    return lax.dot_general(left, right, (((1,), (1,)), ((), ())), preferred_element_type=F32)
+
+
+def contract_rows(left, right):
+    return lax.dot_general(left, right, (((0,), (0,)), ((), ())), preferred_element_type=F32)
+
+def row_block(step, near_count):
+    return lax.rem(step + near_count, CORES * near_count)
+
+
+def send_rows(step, near_count, mp_at, held_ref, other_refs, mine_refs):
+    count = len(other_refs)
+    own_rows = held_ref.shape[0] // count
+
+    def write(refs):
+        for away, ref in enumerate(refs):
+            first = pl.multiple_of(lax.bitwise_xor(mp_at, away) * own_rows, own_rows)
+            ref[0] = held_ref[pl.ds(first, own_rows), :]
+
+    @pl.when(step < near_count)
+    def _():
+        write(other_refs)
+
+    @pl.when(step >= near_count)
+    def _():
+        write(mine_refs)
+
+
+def sent_specs(near_count, count, own_rows, model):
+    other = pl.BlockSpec((1, own_rows, model), lambda i: (jnp.minimum(i, near_count - 1), 0, 0))
+    mine = pl.BlockSpec((1, own_rows, model), lambda i: (jnp.maximum(i - near_count, 0), 0, 0))
+    shape = jax.ShapeDtypeStruct((near_count, own_rows, model), LOW)
+    return [other] * count + [mine] * count, [shape] * (2 * count)
+
+
+def partial_kernel(near_count, count, product, place_ref, left_ref, weight_ref, *refs):
+    held_ref = refs[-1]
+    product(left_ref, weight_ref, held_ref)
+    send_rows(
+        pl.program_id(0), near_count, place_ref[3], held_ref, refs[:count], refs[count : 2 * count]
+    )
+
+
+def partial_rows(left, weight, model, place, near_count, count, product, name):
+    seq_len, depth = left.shape
+    rows = seq_len // (CORES * near_count)
+    out_specs, out_shape = sent_specs(near_count, count, rows // count, model)
+    outs = pl.pallas_call(
+        functools.partial(partial_kernel, near_count, count, product),
+        grid=(CORES * near_count,),
+        in_specs=[
+            pl.BlockSpec(memory_space=pltpu.SMEM),
+            pl.BlockSpec((rows, depth), lambda i: (row_block(i, near_count), 0)),
+            pl.BlockSpec(weight.shape, lambda i: (0, 0, 0)),
+        ],
+        out_specs=out_specs,
+        out_shape=out_shape,
+        scratch_shapes=[pltpu.VMEM((rows, model), LOW)],
+        compiler_params=pltpu.CompilerParams(vmem_limit_bytes=40 * 2**20),
+        cost_estimate=pl.CostEstimate(
+            flops=2 * seq_len * depth * model, bytes_accessed=2 * seq_len * model, transcendentals=0
+        ),
+        name=name,
+    )(place, left, weight)
+    return outs[count:], outs[:count]
+
+
+def column_product(shard, first, last, left_ref, weight_ref, held_ref):
+    weight = weight_ref[:, :shard, first:last]
+    weight = weight.reshape(weight.shape[0] * shard, last - first)
+    held_ref[...] = contract_cols(left_ref[...], weight).astype(LOW)
+
+
+def row_product(height, left_ref, weight_ref, held_ref):
+    left = left_ref[...]
+    width = weight_ref.shape[2]
+    for at in range(weight_ref.shape[0]):
+        held_ref[:, at * width : (at + 1) * width] = rows_dot(
+            left, weight_ref[at, :height, :]
+        ).astype(LOW)
+
+
+def ffn_blocks_kernel(seqs, members, gate_ref, up_ref, down_ref, gain_ref, first_ref, second_ref):
+    shard = gate_ref.shape[0]
+    width = gate_ref.shape[1] // members
+    gain = as_column(gain_ref[...].astype(LOW).astype(F32), 0, shard)
+    for member in range(members):
+        here = slice(member * width, (member + 1) * width)
+        parts = [
+            (ref[:, here].astype(LOW).astype(F32) * gain).astype(LOW) for ref in (gate_ref, up_ref)
+        ]
+        both = jnp.concatenate(parts, 1)
+        down = down_ref[here, :].astype(LOW)
+        for seq in range(seqs):
+            at = seq * members + member
+            first_ref[at, :width, :] = down
+            first_ref[at, width:, :] = both[:, :shard]
+            second_ref[at] = both[:, shard:]
+
+
+def ffn_blocks(w_gate, w_up, w_down, gain, seqs, members):
+    shard, columns = w_gate.shape
+    width = columns // members
+    return pl.pallas_call(
+        functools.partial(ffn_blocks_kernel, seqs, members),
+        out_shape=[
+            jax.ShapeDtypeStruct((seqs * members, width + shard, shard), LOW),
+            jax.ShapeDtypeStruct((seqs * members, shard, 2 * width - shard), LOW),
+        ],
+        compiler_params=pltpu.CompilerParams(vmem_limit_bytes=40 * 2**20),
+        cost_estimate=pl.CostEstimate(
+            flops=0, bytes_accessed=18 * shard * columns, transcendentals=0
+        ),
+        name="ffn_blocks",
+    )(w_gate, w_up, w_down, gain)
+
+
+def ffn_kernel(
+    near_count, count, place_ref, rows_ref, grad_ref, first_ref, second_ref, *refs
+):
+    other_refs, mine_refs = refs[:count], refs[count : 2 * count]
+    act_ref, d_ref, down_ref, held_ref, sum_ref = refs[2 * count :]
+    step = pl.program_id(0)
+    sources, height, shard = first_ref.shape
+    width = height - shard
+    rows = rows_ref[...]
+    grads = grad_ref[...]
+    early = first_ref[:, width:, :].reshape(sources * shard, shard)
+    late = second_ref[...].reshape(sources * shard, 2 * width - shard)
+    both = jnp.concatenate([rows_dot(rows, early), rows_dot(rows, late)], 1)
+    gate, up = both[:, :width], both[:, width:]
+    scale, cubic = 0.7978845608028654, 0.044715
+    square = gate * gate
+    bent = jnp.tanh(scale * (gate + cubic * square * gate))
+    half = 0.5 * (1.0 + bent)
+    value = gate * half
+    slope = half + 0.5 * gate * (1.0 - bent * bent) * (scale * (1.0 + 3.0 * cubic * square))
+    act = (value * up).astype(LOW)
+    act_ref[...] = act
+    d_hidden = jnp.zeros((rows.shape[0], width), F32)
+    for at in range(sources):
+        d_hidden = d_hidden + contract_cols(
+            grads[:, at * shard : (at + 1) * shard], first_ref[at, :width, :]
+        )
+    d_both = jnp.concatenate(
+        [(d_hidden * up * slope).astype(LOW), (d_hidden * value).astype(LOW)], 1
+    )
+    d_ref[...] = d_both
+    held_ref[...] = (
+        contract_cols(d_both[:, :shard], early) + contract_cols(d_both[:, shard:], late)
+    ).astype(LOW)
+    send_rows(step, near_count, place_ref[3], held_ref, other_refs, mine_refs)
+    product = contract_rows(act, grads)
+
+    @pl.when(step == 0)
+    def _():
+        sum_ref[...] = product
+
+    @pl.when(step > 0)
+    def _():
+        sum_ref[...] += product
+
+    @pl.when(step == pl.num_programs(0) - 1)
+    def _():
+        for at in range(sources):
+            down_ref[at] = sum_ref[:, at * shard : (at + 1) * shard].astype(LOW)
+
+
+def feed_forward(rows_all, grads, first, second, place, near_count, count):
+    seq_len, model = rows_all.shape
+    sources, height, shard = first.shape
+    width = height - shard
+    rows = seq_len // (CORES * near_count)
+    out_specs, out_shape = sent_specs(near_count, count, rows // count, model)
+
+    def blocks(columns):
+        return pl.BlockSpec((rows, columns), lambda i: (row_block(i, near_count), 0))
+
+    outs = pl.pallas_call(
+        functools.partial(ffn_kernel, near_count, count),
+        grid=(CORES * near_count,),
+        in_specs=[
+            pl.BlockSpec(memory_space=pltpu.SMEM),
+            blocks(model),
+            blocks(model),
+            pl.BlockSpec(first.shape, lambda i: (0, 0, 0)),
+            pl.BlockSpec(second.shape, lambda i: (0, 0, 0)),
+        ],
+        out_specs=out_specs
+        + [
+            blocks(width),
+            blocks(2 * width),
+            pl.BlockSpec((sources, width, shard), lambda i: (0, 0, 0)),
+        ],
+        out_shape=out_shape
+        + [
+            jax.ShapeDtypeStruct((seq_len, width), LOW),
+            jax.ShapeDtypeStruct((seq_len, 2 * width), LOW),
+            jax.ShapeDtypeStruct((sources, width, shard), LOW),
+        ],
+        scratch_shapes=[pltpu.VMEM((rows, model), LOW), pltpu.VMEM((width, model), F32)],
+        compiler_params=pltpu.CompilerParams(vmem_limit_bytes=52 * 2**20),
+        cost_estimate=pl.CostEstimate(
+            flops=12 * seq_len * model * width, bytes_accessed=12 * seq_len * model, transcendentals=0
+        ),
+        name="feed_forward",
+    )(place, rows_all, grads, first, second)
+    return outs[count : 2 * count], outs[:count], *outs[2 * count :]
+
+
 COLUMN = ("seq", "near", "core")
 
 
@@ -385,28 +600,12 @@
     return lax.optimization_barrier((value,) + done)[0]
 
 
-def rows_dot(left, right):
-    return jnp.dot(left, right, preferred_element_type=F32)
-
-
-def contract_cols(left, right):
-    return lax.dot_general(left, right, (((1,), (1,)), ((), ())), preferred_element_type=F32)
-
-
-def contract_rows(left, right):
-    return lax.dot_general(left, right, (((0,), (0,)), ((), ())), preferred_element_type=F32)
-
-
 def rms(values):
     return lax.rsqrt(jnp.mean(values * values, axis=-1, keepdims=True) + EPSILON)
 
 
 def norm_grad(inner, normed, inverse):
     return inverse * (inner - normed * jnp.mean(inner * normed, axis=-1, keepdims=True))
-
-
-def gelu_tanh(values):
-    return jax.nn.gelu(values, approximate=True)
 
 
 def local(
@@ -445,19 +644,9 @@
     mp_at = lax.axis_index("mp")
     member_at = near_at * CORES + core_at
     length = lax.dynamic_slice_in_dim(lengths, lax.axis_index("seq"), 1, 0)
-    place = jnp.stack([length[0], core_at.astype(jnp.int32), member_at.astype(jnp.int32)])
-
-    def for_column(parts):
-        return jnp.broadcast_to(parts[None], (seqs,) + parts.shape).reshape(
-            (sources,) + parts.shape[1:]
-        )
-
-    def by_member(weight):
-        return weight.reshape(weight.shape[0], members, -1)
-
-    def scaled(weight, gain):
-        low = weight.astype(LOW).astype(F32)
-        return (low * gain.astype(LOW).astype(F32)[:, None]).astype(LOW)
+    place = jnp.stack(
+        [length[0]] + [at.astype(jnp.int32) for at in (core_at, member_at, mp_at)]
+    )
 
     def over_mp(own, axis):
         shape = own.shape[:axis] + (mp_count,) + own.shape[axis:]
@@ -482,29 +671,22 @@
 
     def gather_rows(near):
         blocks = [(0, near)] + [(away, shifted(near, away)) for away in range(1, mp_count)]
-        shape = (near_count, mp_count, own_rows, model)
-        mine, other = jnp.zeros(shape, near.dtype), jnp.zeros(shape, near.dtype)
+        rows = jnp.zeros((CORES, near_count, mp_count, own_rows, model), near.dtype)
         for away, block in blocks:
-            at = mp_at ^ away
-            mine = lax.dynamic_update_index_in_dim(mine, block, at, 1)
-            other = lax.dynamic_update_index_in_dim(other, swap(block, "core"), at, 1)
-        return mine.reshape(half_rows, model), other.reshape(half_rows, model)
+            for other, part in enumerate((block, swap(block, "core"))):
+                rows = lax.dynamic_update_slice(
+                    rows, part[None, :, None], (other, 0, mp_at ^ away, 0, 0)
+                )
+        return rows.reshape(seq_len, model), [block for _, block in blocks[1:]]
 
     def sum_cores(mine, other):
-        mine = mine.reshape(near_count, mp_count, own_rows, model)
-        other = other.astype(LOW).reshape(near_count, mp_count, own_rows, model)
-        sums = []
-        for away in reversed(range(mp_count)):
-            at = mp_at ^ away
-            arrived = swap(lax.dynamic_index_in_dim(other, at, 1, keepdims=False), "core")
-            kept = lax.dynamic_index_in_dim(mine, at, 1, keepdims=False)
-            sums.append(kept.astype(F32) + arrived.astype(F32))
-        return sums
+        return [
+            kept.astype(F32) + swap(sent, "core").astype(F32) for kept, sent in zip(mine, other)
+        ]
 
     def send_mp(sums):
-        last = len(sums) - 1
-        moved = [shifted(rows.astype(LOW), last - i) for i, rows in enumerate(sums[:-1])]
-        return moved, sums[-1]
+        moved = [shifted(sums[away].astype(LOW), away) for away in reversed(range(1, mp_count))]
+        return moved, sums[0]
 
     def sum_mp(sums):
         moved, kept = send_mp(sums)
@@ -530,21 +712,18 @@
     attn_sent = attention_blocks(
         (w_query, w_key, w_value), w_out, attn_scale.reshape(1, shard), rel_table, seqs, members
     )
-    gate_up_parts = for_column(
-        jnp.moveaxis(
-            jnp.concatenate(
-                [by_member(scaled(w_gate, ffn_scale)), by_member(scaled(w_up, ffn_scale))], 2
-            ),
-            1,
-            0,
-        )
-    )
-    down_parts = for_column(w_down.astype(LOW).reshape(members, hidden_width, shard))
+    ffn_first, ffn_second = ffn_blocks(
+        w_gate, w_up, w_down, ffn_scale.reshape(1, shard), seqs, members
+    )
 
     attn_got = exchange(attn_sent, COLUMN)
     attn_weights = attn_got[:, :shard].reshape(model, 4 * width)
     qkv_weight = attn_weights[:, : 3 * width]
     out_weight_t = attn_weights[:, 3 * width :]
+
+    def partial(left, weight, product, name):
+        return partial_rows(left, weight, model, place, near_count, mp_count, product, name)
+
     table = attn_got[:, shard : shard + table_rows, :heads_mp].reshape(buckets, heads_mp)
 
     mine_inputs = near_block_rows(inputs)
@@ -554,53 +733,33 @@
     row_valid = (member_at * tok_rows + lax.iota(jnp.int32, tok_rows) < length)[:, None]
     masked = jnp.where(row_valid, cotangent, jnp.zeros_like(cotangent))
     mine_grad = near_block_rows(masked)
-    other_grad = swap(mine_grad, "core")
-
-    normed_rows = after(normed_rows, gate_up_parts, down_parts)
-    down_got = exchange(after(down_parts, attn_got), COLUMN)
-    down_weight = jnp.moveaxis(down_got, 0, 1).reshape(hidden_width, model)
+    grad_two = jnp.concatenate([mine_grad, swap(mine_grad, "core")], 0)
+
+    normed_rows = after(normed_rows, ffn_first, ffn_second)
+    first_got = exchange(after(ffn_first, attn_got), COLUMN)
 
     qkv = rows_dot(normed_rows, qkv_weight).astype(LOW)
     attended, prob = attention_forward(qkv, table, place, heads, tok_rows)
-    attended = after(attended, mine_grad, other_grad)
+    attended = after(attended, mine_grad)
+    out_product = functools.partial(column_product, shard, 3 * width, 4 * width)
     mixed, mixed_moved = sum_near_both(
         after(
-            sum_mp(
-                sum_cores(
-                    contract_cols(attended[:half_rows], out_weight_t),
-                    contract_cols(attended[half_rows:], out_weight_t),
-                )
-            ),
-            down_got,
-        )
-    )
-    gate_up_weight = exchange(after(gate_up_parts, mixed_moved), COLUMN).reshape(model, 2 * hidden_width)
+            sum_mp(sum_cores(*partial(attended, attn_got, out_product, "attention_out"))), first_got
+        )
+    )
+    second_got = exchange(after(ffn_second, mixed_moved), COLUMN)
 
     pair_inputs = near_pair(after(mine_inputs, normed_rows)).astype(F32)
     pair_cotangent = near_pair(mine_grad).astype(F32)
     after_attn = pair_inputs + mixed
     inv_two = rms(after_attn)
     normed_two = after_attn * inv_two
-    halves = gather_rows(normed_two.astype(LOW))
-
-    grads = (mine_grad, other_grad)
-    ups, gelus, acts = [], [], []
-    for rows in halves:
-        gate_up = rows_dot(rows, gate_up_weight)
-        gelus.append(jax.vjp(gelu_tanh, gate_up[:, :hidden_width]))
-        ups.append(gate_up[:, hidden_width:])
-        acts.append((gelus[-1][0] * ups[-1]).astype(LOW))
-    d_down_w = (contract_rows(acts[0], grads[0]) + contract_rows(acts[1], grads[1])).astype(LOW)
-    d_gate_ups, d_norms = [], []
-    for grad, up_pre, (gelu_value, gelu_pull) in zip(grads, ups, gelus):
-        d_hidden = contract_cols(after(grad, d_down_w), down_weight)
-        (d_gate_pre,) = gelu_pull(d_hidden * up_pre)
-        d_gate_ups.append(
-            jnp.concatenate([d_gate_pre.astype(LOW), (d_hidden * gelu_value).astype(LOW)], 1)
-        )
-        d_norms.append(contract_cols(d_gate_ups[-1], gate_up_weight))
-    inner_cores = sum_cores(*d_norms)
-    d_gate_ups = [after(grad, *d_norms) for grad in d_gate_ups]
+    hidden_two, _ = gather_rows(normed_two.astype(LOW))
+
+    d_mine, d_other, acts, d_both, d_down_w = feed_forward(
+        hidden_two, grad_two, first_got, second_got, place, near_count, mp_count
+    )
+    inner_cores = sum_cores(d_mine, d_other)
 
     def to_owners(grad):
         return exchange(grad, COLUMN)
@@ -609,11 +768,9 @@
         parts = got.reshape((seqs, members) + got.shape[1:]).astype(F32)
         return jnp.sum(parts, axis=0).reshape(-1, shard)
 
-    d_down = to_owners(jnp.moveaxis(d_down_w.reshape(hidden_width, sources, shard), 1, 0))
+    d_down = to_owners(d_down_w)
     inner_two, inner_moved = sum_near_both(after(sum_mp(inner_cores), d_down))
-    d_gate_up_w = (
-        contract_rows(halves[0], d_gate_ups[0]) + contract_rows(halves[1], d_gate_ups[1])
-    ).astype(LOW)
+    d_gate_up_w = contract_rows(hidden_two, after(d_both, *inner_cores)).astype(LOW)
     d_gate_up = to_owners(after(d_gate_up_w, inner_moved).reshape(sources, shard, -1))
 
     pair_first = (
@@ -623,17 +780,16 @@
     )
     pair_valid = pair_first < length
     grad_one = pair_cotangent + norm_grad(inner_two, normed_two, inv_two)
-    mine_one, other_one = gather_rows(grad_one.astype(LOW))
-    ffn_cores = sum_cores(*[rows_dot(after(act, inner_moved), down_weight) for act in acts])
-    d_attended = jnp.concatenate(
-        [rows_dot(mine_one, out_weight_t), rows_dot(other_one, out_weight_t)], 0
-    ).astype(LOW)
+    rows_one, came_one = gather_rows(grad_one.astype(LOW))
+    down_product = functools.partial(row_product, hidden_width)
+    ffn_cores = sum_cores(*partial(after(acts, inner_moved), first_got, down_product, "ffn_out"))
+    d_attended = rows_dot(rows_one, out_weight_t).astype(LOW)
     d_qkv, d_table = attention_backward(prob, d_attended, qkv, place, heads, tok_rows, buckets)
+    qkv_product = functools.partial(column_product, shard, 0, 3 * width)
+    ffn_moved, ffn_kept = send_mp([after(rows, *came_one) for rows in ffn_cores])
     inner_cores = sum_cores(
-        contract_cols(d_qkv[:half_rows], qkv_weight), contract_cols(d_qkv[half_rows:], qkv_weight)
-    )
-    ffn_moved, ffn_kept = send_mp([after(rows, mine_one) for rows in ffn_cores])
-    ffn_moved = [after(rows, d_qkv) for rows in ffn_moved]
+        *partial(after(d_qkv, *ffn_moved), attn_got, qkv_product, "attention_in")
+    )
     last_moved, last_kept = send_mp(inner_cores)
     inner_one = sum_near(sum((piece.astype(F32) for piece in last_moved), last_kept))
     table_sent = d_table[:, :heads].astype(LOW).reshape(sources, table_rows, heads)
@@ -643,10 +799,7 @@
     d_qkv_w = contract_rows(normed_rows, d_qkv).astype(LOW).reshape(sources, shard, -1)
     d_qkv_sent = jnp.concatenate([d_qkv_w, table_sent], 1)
     d_qkv_got = to_owners(after(d_qkv_sent, d_gate_up, last_moved[0]))
-    later_attended = after(attended, inner_cores[0])
-    d_out = contract_rows(later_attended[:half_rows], mine_one) + contract_rows(
-        later_attended[half_rows:], other_one
-    )
+    d_out = contract_rows(after(attended, inner_cores[0]), rows_one)
     d_out = jnp.moveaxis(d_out.astype(LOW).reshape(width, sources, shard), 1, 0)
     d_out = to_owners(after(d_out, d_qkv_got))
 
@@ -655,9 +808,9 @@
     grad_input = here(grad_one) + norm_grad(inner_one, normed_one, rms(own_inputs))
     d_inputs = over_mp(grad_input.astype(LOW), 0).reshape(tok_rows, model)
     ffn_pair = sum((piece.astype(F32) for piece in ffn_moved), ffn_kept)
-    after_ffn = here(after_attn) + sum_near(after(ffn_pair, inner_one))
+    after_ffn = here(after_attn) + sum_near(after(ffn_pair, d_qkv_got))
     own_out = jnp.where(here(pair_valid), after_ffn, 0.0).astype(LOW)
-    layer_out = over_mp(after(own_out, d_qkv_got), 0).reshape(tok_rows, model)
+    layer_out = over_mp(own_out, 0).reshape(tok_rows, model)
 
     (d_w_gate, d_w_up), ffn_gain, _ = owner_grads(
         after(d_gate_up, inner_cores[0]), (w_gate, w_up), ffn_scale.reshape(1, shard), members, None

time: 477 us -> 470 us (0.985)
  matrix products: 59.6 us -> 16.7 us
  Pallas kernels: 30.6 us -> 61.1 us
  waiting for transfers between devices: 195 us -> 208 us
  local copies, waits for them, and re-layouts: 50.5 us -> 38 us
  other arithmetic: 41.6 us -> 53 us
    pallas_call x0 -> x5, Pallas kernels: none -> 32.4 us  [the longest x1 18.3 us: feed_forward(): pl.pallas_call(functools.partial(ffn_kernel, near_count, count), grid=(CO...]
    dot_general x8 -> x0, matrix products: 22.7 us -> none  [contract_cols(): lax.dot_general(left, right, (((1,), (1,)), ((), ())), preferred_element_...]
    ppermute x32, waiting for transfers between devices: 44.1 us -> 54.5 us  [swap(): return lax.ppermute(block, axis, [(0, 1), (1, 0)])]
    dot_general x7 -> x3, matrix products: 20.9 us -> 10.6 us  [contract_rows(): lax.dot_general(left, right, (((0,), (0,)), ((), ())), preferred_element_...]
    dot_general x7 -> x2, matrix products: 16 us -> 6.1 us  [rows_dot(): return jnp.dot(left, right, preferred_element_type=F32)]
    reshape x3 -> x0, local copies, waits for them, and re-layouts: 5.7 us -> none  [the longest x2 4.56 us: local(): down_weight = jnp.moveaxis(down_got, 0, 1).reshape(hidden_width, model)]
    all_to_all x7, waiting for transfers between devices: 31.7 us -> 37.1 us  [exchange(): return lax.all_to_all(blocks, axes, split_axis=0, concat_axis=0, tiled=True)]
    unnamed x107 -> x95, local copies, waits for them, and re-layouts: 11.4 us -> 14.8 us
  transfers between devices with their start and end apart: 72 -> 72, of which waited for: 35 -> 31; matrix products, arithmetic and copies ran while one was open for 22% -> 18% of each run, Pallas kernels for 6% -> 9%
where the time goes in v2:
time: 470 us; the launch traced here: 464 us
  waiting for transfers between devices  208 us (44%)
  starting transfers between devices  86.1 us (18%)
  Pallas kernels  61.1 us (13%)
  other arithmetic  53 us (11%)
  local copies, waits for them, and re-layouts  38 us (8%)
  matrix products  16.7 us (4%)
    ppermute x33, waiting for transfers between devices, shifted(): return lax.ppermute(block, 'mp', [(i, i ^ away) for i in range(mp_count)])  116 us
    ppermute x32, waiting for transfers between devices, swap(): return lax.ppermute(block, axis, [(0, 1), (1, 0)])  54.5 us
    ppermute x33, starting transfers between devices, shifted(): return lax.ppermute(block, 'mp', [(i, i ^ away) for i in range(mp_count)])  40.3 us
    all_to_all x7, waiting for transfers between devices, exchange(): return lax.all_to_all(blocks, axes, split_axis=0, concat_axis=0, tiled=True)  37.1 us
    all_to_all x7, starting transfers between devices, exchange(): return lax.all_to_all(blocks, axes, split_axis=0, concat_axis=0, tiled=True)  32 us
    pallas_call x1, Pallas kernels, feed_forward(): pl.pallas_call(functools.partial(ffn_kernel, near_count, count), grid=(CO...  18.3 us
    unnamed x95, local copies, waits for them, and re-layouts  14.8 us
    ppermute x32, starting transfers between devices, swap(): return lax.ppermute(block, axis, [(0, 1), (1, 0)])  13.9 us
  transfers between devices with their start and end apart: 72, of which 31 were waited for; matrix products, arithmetic and copies ran while one was open for 18% of the time, Pallas kernels for 9%

profile of v2, /device:TPU:0, one launch (start us, length us, event | category | flops | bytes accessed | tf_op | source)
XLA Modules:
  0.0 464.4 jit_solution(18175086528237086989)
XLA Ops:
  16.5 5.3 %all-to-all-start = ((bf16[8,264,512]{2,1,0:T(8,128)(2,1)}), bf16[8,264,512]{2,1,0:T(8,128)(2,1)S(1)}, u32[]{:S(2)}, u32[]{:S(2)}) async-start(bf16[8,264,512]{2,1,0:T(8,128)(2,1)} %copy-done.2), calls=%async_computation | async-start | bytes 4325376 | tf_op jit(solution)/shard_map/all_to_all | solution.py:592
  37.6 5.2 %collective-permute-done.7 = bf16[64,2048]{1,0:T(8,128)(2,1)S(1)} collective-permute-done((bf16[64,2048]{1,0:T(8,128)(2,1)S(1)}, bf16[64,2048]{1,0:T(8,128)(2,1)S(1)}, u32[]{:S(2)}, u32[]{:S(2)}) %collective-permute-start.7) | collective-permute-done | bytes 262176 | tf_op jit(solution)/shard_map/ppermute | solution.py:660
  42.8 5.5 %collective-permute-done.2 = bf16[64,2048]{1,0:T(8,128)(2,1)S(1)} collective-permute-done((bf16[64,2048]{1,0:T(8,128)(2,1)S(1)}, bf16[64,2048]{1,0:T(8,128)(2,1)S(1)}, u32[]{:S(2)}, u32[]{:S(2)}) %collective-permute-start.2) | collective-permute-done | bytes 262176 | tf_op jit(solution)/shard_map/ppermute | solution.py:660
  59.4 12.9 %all-to-all-done.weight_ref = bf16[8,264,512]{2,1,0:T(8,128)(2,1)S(1)} async-done(((bf16[8,264,512]{2,1,0:T(8,128)(2,1)}), bf16[8,264,512]{2,1,0:T(8,128)(2,1)S(1)}, u32[]{:S(2)}, u32[]{:S(2)}) %all-to-all-start) | async-done | bytes 2162720 | tf_op jit(solution)/shard_map/all_to_all | solution.py:592
  85.8 7.4 %attention_forward.1 = (bf16[1024,128]{1,0:T(8,128)(2,1)S(1)}, bf16[2,1024,1024]{2,1,0:T(8,128)(2,1)S(1)}) custom-call(s32[4]{0:T(128)S(1)} %pad_add_fusion.place_ref, bf16[1024,384]{1,0:T(8,128)(2,1)S(1)} %fusion.4.qkv_ref, bf16[32,8]{1,0:T(8,128)(2,1)S(1)} %bitcast.207), custom_call_target="tpu_custom_call" | custom-call | flops 536870912 | bytes 4194304 | tf_op jit(solution)/shard_map/attention_forward/pallas_call | solution.py:121
  104.0 11.7 %collective-permute-done.11 = bf16[2,64,2048]{2,1,0:T(8,128)(2,1)S(1)} collective-permute-done((bf16[2,64,2048]{2,1,0:T(8,128)(2,1)S(1)}, bf16[2,64,2048]{2,1,0:T(8,128)(2,1)S(1)}, u32[]{:S(2)}, u32[]{:S(2)}) %collective-permute-start.11) | collective-permute-done | bytes 524320 | tf_op jit(solution)/shard_map/ppermute | solution.py:660
  115.7 10.6 %collective-permute-done.13 = bf16[2,64,2048]{2,1,0:T(8,128)(2,1)S(1)} collective-permute-done((bf16[2,64,2048]{2,1,0:T(8,128)(2,1)S(1)}, bf16[2,64,2048]{2,1,0:T(8,128)(2,1)S(1)}, u32[]{:S(2)}, u32[]{:S(2)}) %collective-permute-start.13) | collective-permute-done | bytes 524320 | tf_op jit(solution)/shard_map/ppermute | solution.py:660
  126.9 5.0 %all-to-all-done.1.first_ref.weight_ref = bf16[8,576,256]{2,1,0:T(8,128)(2,1)} async-done(((bf16[8,576,256]{2,1,0:T(8,128)(2,1)}), bf16[8,576,256]{2,1,0:T(8,128)(2,1)}, u32[]{:S(2)}, u32[]{:S(2)}) %all-to-all-start.1) | async-done | bytes 2359328 | tf_op jit(solution)/shard_map/all_to_all | solution.py:592
  131.9 13.5 %collective-permute-done.16 = bf16[2,64,2048]{2,1,0:T(8,128)(2,1)S(1)} collective-permute-done((bf16[2,64,2048]{2,1,0:T(8,128)(2,1)S(1)}, bf16[2,64,2048]{2,1,0:T(8,128)(2,1)S(1)}, u32[]{:S(2)}, u32[]{:S(2)}) %collective-permute-start.16) | collective-permute-done | bytes 524320 | tf_op jit(solution)/shard_map/ppermute | solution.py:596
  165.5 10.2 %collective-permute-done.20 = bf16[2,64,2048]{2,1,0:T(8,128)(2,1)S(1)} collective-permute-done((bf16[2,64,2048]{2,1,0:T(8,128)(2,1)}, bf16[2,64,2048]{2,1,0:T(8,128)(2,1)S(1)}, u32[]{:S(2)}, u32[]{:S(2)}) %collective-permute-start.20) | collective-permute-done | bytes 524320 | tf_op jit(solution)/shard_map/ppermute | solution.py:660
  183.1 18.0 %all-to-all-done.2.second_ref = bf16[8,256,384]{2,1,0:T(8,128)(2,1)} async-done(((bf16[8,256,384]{2,1,0:T(8,128)(2,1)}), bf16[8,256,384]{2,1,0:T(8,128)(2,1)}, u32[]{:S(2)}, u32[]{:S(2)}) %all-to-all-start.2) | async-done | bytes 1572896 | tf_op jit(solution)/shard_map/all_to_all | solution.py:592
  201.1 18.3 %feed_forward.1 = (bf16[2,64,2048]{2,1,0:T(8,128)(2,1)S(1)}, bf16[2,64,2048]{2,1,0:T(8,128)(2,1)S(1)}, bf16[2,64,2048]{2,1,0:T(8,128)(2,1)S(1)}, bf16[2,64,2048]...) custom-call(s32[4]{0:T(128)S(1)} %pad_add_fusion.place_ref, ...), custom_call_target="tpu_custom_call" | custom-call | flops 8053063680 | bytes 25165824 | tf_op jit(solution)/shard_map/feed_forward/pallas_call | solution.py:556
  233.8 9.1 %collective-permute-done.27 = bf16[2,64,2048]{2,1,0:T(8,128)(2,1)} collective-permute-done((bf16[2,64,2048]{2,1,0:T(8,128)(2,1)}, bf16[2,64,2048]{2,1,0:T(8,128)(2,1)}, u32[]{:S(2)}, u32[]{:S(2)}) %collective-permute-start.27) | collective-permute-done | bytes 524320 | tf_op jit(solution)/shard_map/ppermute | solution.py:660
  242.9 10.6 %collective-permute-done.29 = bf16[2,64,2048]{2,1,0:T(8,128)(2,1)} collective-permute-done((bf16[2,64,2048]{2,1,0:T(8,128)(2,1)S(1)}, bf16[2,64,2048]{2,1,0:T(8,128)(2,1)}, u32[]{:S(2)}, u32[]{:S(2)}) %collective-permute-start.29) | collective-permute-done | bytes 524320 | tf_op jit(solution)/shard_map/ppermute | solution.py:660
  260.2 10.2 %collective-permute-done.32 = bf16[2,64,2048]{2,1,0:T(8,128)(2,1)S(1)} collective-permute-done((bf16[2,64,2048]{2,1,0:T(8,128)(2,1)S(1)}, bf16[2,64,2048]{2,1,0:T(8,128)(2,1)S(1)}, u32[]{:S(2)}, u32[]{:S(2)}) %collective-permute-start.32) | collective-permute-done | bytes 524320 | tf_op jit(solution)/shard_map/ppermute | solution.py:596
  276.3 5.7 %ffn_out.1 = (bf16[2,64,2048]{2,1,0:T(8,128)(2,1)S(1)}, bf16[2,64,2048]{2,1,0:T(8,128)(2,1)S(1)}, bf16[2,64,2048]{2,1,0:T(8,128)(2,1)}, bf16[2,64,2048]{2,1,0:T(...) custom-call(s32[4]{0:T(128)S(1)} %pad_add_fusion.place_ref, ...), custom_call_target="tpu_custom_call" | custom-call | flops 1342177280 | bytes 4194304 | tf_op jit(solution)/shard_map/ffn_out/pallas_call | solution.py:425
  282.6 7.5 %convolution_convert_fusion = bf16[2048,640]{1,0:T(8,128)(2,1)} fusion(bf16[1024,2048]{1,0:T(8,128)(2,1)} %bitcast.44.rows_ref, bf16[1024,640]{1,0:T(8,128)(2,1)S(1)} %copy-done.46), kind=kOutput, calls=%fused_computation.6 | convolution fusion | flops 2685665280 | bytes 8126464 | tf_op jit(solution)/shard_map/dot_general | solution.py:382
  312.1 12.1 %attention_backward.1 = (bf16[1024,384]{1,0:T(8,128)(2,1)S(1)}, f32[32,128]{1,0:T(8,128)S(1)}) custom-call(s32[4]{0:T(128)S(1)} %pad_add_fusion.place_ref, bf16[2,1024,1024]{2,1,0:T(8,128)(2,1)S(1)} %copy-done.27, bf16[1024,128]{1,0:T(8,128)(2,1)S(1)} %convolution_convert_fusion.3.do_ref, bf16[1024,384]{1,0:T(8,128)(2,1)S(1)} %copy-done.29), custom_call_target="tpu_custom_call" | custom-call | flops 4294967296 | bytes 4194304 | tf_op jit(solution)/shard_map/attention_backward/pallas_call | solution.py:221
  341.7 10.6 %collective-permute-done.48 = bf16[2,64,2048]{2,1,0:T(8,128)(2,1)S(1)} collective-permute-done((bf16[2,64,2048]{2,1,0:T(8,128)(2,1)S(1)}, bf16[2,64,2048]{2,1,0:T(8,128)(2,1)S(1)}, u32[]{:S(2)}, u32[]{:S(2)}) %collective-permute-start.48) | collective-permute-done | bytes 524320 | tf_op jit(solution)/shard_map/ppermute | solution.py:660
  352.3 10.3 %collective-permute-done.55 = bf16[2,64,2048]{2,1,0:T(8,128)(2,1)S(1)} collective-permute-done((bf16[2,64,2048]{2,1,0:T(8,128)(2,1)S(1)}, bf16[2,64,2048]{2,1,0:T(8,128)(2,1)S(1)}, u32[]{:S(2)}, u32[]{:S(2)}) %collective-permute-start.55) | collective-permute-done | bytes 524320 | tf_op jit(solution)/shard_map/ppermute | solution.py:660
  371.9 29.3 %collective-permute-done.58 = bf16[64,2048]{1,0:T(8,128)(2,1)S(1)} collective-permute-done((bf16[64,2048]{1,0:T(8,128)(2,1)S(1)}, bf16[64,2048]{1,0:T(8,128)(2,1)S(1)}, u32[]{:S(2)}, u32[]{:S(2)}) %collective-permute-start.58) | collective-permute-done | bytes 262176 | tf_op jit(solution)/shard_map/ppermute | solution.py:596
  411.5 5.3 %collective-permute-done.59 = bf16[64,2048]{1,0:T(8,128)(2,1)S(1)} collective-permute-done((bf16[64,2048]{1,0:T(8,128)(2,1)}, bf16[64,2048]{1,0:T(8,128)(2,1)S(1)}, u32[]{:S(2)}, u32[]{:S(2)}) %collective-permute-start.59) | collective-permute-done | bytes 262176 | tf_op jit(solution)/shard_map/ppermute | solution.py:660
  451.8 6.0 %collective-permute-done.50 = bf16[64,2048]{1,0:T(8,128)(2,1)S(1)} collective-permute-done((bf16[64,2048]{1,0:T(8,128)(2,1)S(1)}, bf16[64,2048]{1,0:T(8,128)(2,1)S(1)}, u32[]{:S(2)}, u32[]{:S(2)}) %collective-permute-start.50) | collective-permute-done | bytes 262176 | tf_op jit(solution)/shard_map/ppermute | solution.py:660
  457.8 5.2 %collective-permute-done.51 = bf16[64,2048]{1,0:T(8,128)(2,1)S(1)} collective-permute-done((bf16[64,2048]{1,0:T(8,128)(2,1)S(1)}, bf16[64,2048]{1,0:T(8,128)(2,1)S(1)}, u32[]{:S(2)}, u32[]{:S(2)}) %collective-permute-start.51) | collective-permute-done | bytes 262176 | tf_op jit(solution)/shard_map/ppermute | solution.py:660
  (323 shorter events, 217.0 us)
Async XLA Ops:
  16.5 55.8 %all-to-all-start = ((bf16[8,264,512]{2,1,0:T(8,128)(2,1)}), bf16[8,264,512]{2,1,0:T(8,128)(2,1)S(1)}, u32[]{:S(2)}, u32[]{:S(2)}) async-start(bf16[8,264,512]{2,1,0:T(8,128)(2,1)} %copy-done.2), calls=%async_computation | async-start | bytes 4325376 | tf_op jit(solution)/shard_map/all_to_all | solution.py:592
  52.4 27.9 %collective-permute-start.4 = (bf16[512,2048]{1,0:T(8,128)(2,1)}, bf16[512,2048]{1,0:T(8,128)(2,1)}, u32[]{:S(2)}, u32[]{:S(2)}) collective-permute-start(bf16[512,2048]{1,0:T(8,128)(2,1)} %multiply_convert_fusion), channel_id=1, source_target_pairs={{0,4},{4,0},{1,5},{5,1},{2,6},{6,2},{3,7},{7,3},{8,12},{12,8},{9,1... | collective-permute-start | bytes 6291464 | tf_op jit(solution)/shard_map/ppermute | solution.py:596
  72.3 59.6 %all-to-all-start.1 = ((bf16[8,576,256]{2,1,0:T(8,128)(2,1)}), bf16[8,576,256]{2,1,0:T(8,128)(2,1)}, u32[]{:S(2)}, u32[]{:S(2)}) async-start(bf16[8,576,256]{2,1,0:T(8,128)(2,1)} %copy-done.7), calls=%async_computation.1 | async-start | bytes 4718592 | tf_op jit(solution)/shard_map/all_to_all | solution.py:592
  102.6 23.7 %collective-permute-start.13 = (bf16[2,64,2048]{2,1,0:T(8,128)(2,1)S(1)}, bf16[2,64,2048]{2,1,0:T(8,128)(2,1)S(1)}, u32[]{:S(2)}, u32[]{:S(2)}) collective-permute-start(bf16[2,64,2048]{2,1,0:T(8,128)(2,1)S(1)} %add_convert_fusion.4), channel_id=1, source_target_pairs={{0,2},{1,3},{2,0},{3,1},{4,6},{5,7},{6,4},{7,5},{8,10},{9,11},{10,... | collective-permute-start | bytes 1572872 | tf_op jit(solution)/shard_map/ppermute | solution.py:660
  103.3 23.1 %collective-permute-start.15 = (bf16[2,64,2048]{2,1,0:T(8,128)(2,1)S(1)}, bf16[2,64,2048]{2,1,0:T(8,128)(2,1)S(1)}, u32[]{:S(2)}, u32[]{:S(2)}) collective-permute-start(bf16[2,64,2048]{2,1,0:T(8,128)(2,1)S(1)} %add_convert_fusion.3), channel_id=1, source_target_pairs={{0,1},{1,0},{2,3},{3,2},{4,5},{5,4},{6,7},{7,6},{8,9},{9,8},{10,11... | collective-permute-start | bytes 1572872 | tf_op jit(solution)/shard_map/ppermute | solution.py:660
  104.0 49.9 %collective-permute-start.24 = (bf16[512,2048]{1,0:T(8,128)(2,1)}, bf16[512,2048]{1,0:T(8,128)(2,1)}, u32[]{:S(2)}, u32[]{:S(2)}) collective-permute-start(bf16[512,2048]{1,0:T(8,128)(2,1)} %bitcast.26), channel_id=1, source_target_pairs={{0,4},{4,0},{1,5},{5,1},{2,6},{6,2},{3,7},{7,3},{8,12},{12,8},{9,1... | collective-permute-start | bytes 6291464 | tf_op jit(solution)/shard_map/ppermute | solution.py:596
  151.9 23.7 %collective-permute-start.20 = (bf16[2,64,2048]{2,1,0:T(8,128)(2,1)}, bf16[2,64,2048]{2,1,0:T(8,128)(2,1)S(1)}, u32[]{:S(2)}, u32[]{:S(2)}) collective-permute-start(bf16[2,64,2048]{2,1,0:T(8,128)(2,1)} %get-tuple-element.160), channel_id=1, source_target_pairs={{0,2},{1,3},{2,0},{3,1},{4,6},{5,7},{6,4},{7,5},{8,10},{9,11},{10,... | collective-permute-start | bytes 1572872 | tf_op jit(solution)/shard_map/ppermute | solution.py:660
  153.4 22.2 %collective-permute-start.22 = (bf16[2,64,2048]{2,1,0:T(8,128)(2,1)}, bf16[2,64,2048]{2,1,0:T(8,128)(2,1)S(1)}, u32[]{:S(2)}, u32[]{:S(2)}) collective-permute-start(bf16[2,64,2048]{2,1,0:T(8,128)(2,1)} %get-tuple-element.160), channel_id=1, source_target_pairs={{0,3},{1,2},{2,1},{3,0},{4,7},{5,6},{6,5},{7,4},{8,11},{9,10},{10,... | collective-permute-start | bytes 1572872 | tf_op jit(solution)/shard_map/ppermute | solution.py:660
  153.9 22.3 %collective-permute-start.17 = (bf16[2,64,2048]{2,1,0:T(8,128)(2,1)}, bf16[2,64,2048]{2,1,0:T(8,128)(2,1)}, u32[]{:S(2)}, u32[]{:S(2)}) collective-permute-start(bf16[2,64,2048]{2,1,0:T(8,128)(2,1)} %get-tuple-element.160), channel_id=1, source_target_pairs={{0,4},{4,0},{1,5},{5,1},{2,6},{6,2},{3,7},{7,3},{8,12},{12,8},{9,1... | collective-permute-start | bytes 1572872 | tf_op jit(solution)/shard_map/ppermute | solution.py:596
  158.8 42.3 %all-to-all-start.2 = ((bf16[8,256,384]{2,1,0:T(8,128)(2,1)}), bf16[8,256,384]{2,1,0:T(8,128)(2,1)}, u32[]{:S(2)}, u32[]{:S(2)}) async-start(bf16[8,256,384]{2,1,0:T(8,128)(2,1)} %get-tuple-element.98), calls=%async_computation.2 | async-start | bytes 3145728 | tf_op jit(solution)/shard_map/all_to_all | solution.py:592
  220.4 36.5 %all-to-all-start.3 = ((bf16[8,320,256]{2,1,0:T(8,128)(2,1)}), bf16[8,320,256]{2,1,0:T(8,128)(2,1)}, u32[]{:S(2)}, u32[]{:S(2)}) async-start(bf16[8,320,256]{2,1,0:T(8,128)(2,1)} %get-tuple-element.108), calls=%async_computation.3 | async-start | bytes 2621440 | tf_op jit(solution)/shard_map/all_to_all | solution.py:592
  230.7 22.8 %collective-permute-start.29 = (bf16[2,64,2048]{2,1,0:T(8,128)(2,1)S(1)}, bf16[2,64,2048]{2,1,0:T(8,128)(2,1)}, u32[]{:S(2)}, u32[]{:S(2)}) collective-permute-start(bf16[2,64,2048]{2,1,0:T(8,128)(2,1)S(1)} %fusion.19), channel_id=1, source_target_pairs={{0,2},{1,3},{2,0},{3,1},{4,6},{5,7},{6,4},{7,5},{8,10},{9,11},{10,... | collective-permute-start | bytes 1572872 | tf_op jit(solution)/shard_map/ppermute | solution.py:660
  272.8 23.7 %collective-permute-start.34 = (bf16[2,64,2048]{2,1,0:T(8,128)(2,1)}, bf16[2,64,2048]{2,1,0:T(8,128)(2,1)}, u32[]{:S(2)}, u32[]{:S(2)}) collective-permute-start(bf16[2,64,2048]{2,1,0:T(8,128)(2,1)} %get-tuple-element.157), channel_id=1, source_target_pairs={{0,1},{1,0},{2,3},{3,2},{4,5},{5,4},{6,7},{7,6},{8,9},{9,8},{10,11... | collective-permute-start | bytes 1572872 | tf_op jit(solution)/shard_map/ppermute | solution.py:660
  274.3 23.8 %collective-permute-start.35 = (bf16[2,64,2048]{2,1,0:T(8,128)(2,1)}, bf16[2,64,2048]{2,1,0:T(8,128)(2,1)}, u32[]{:S(2)}, u32[]{:S(2)}) collective-permute-start(bf16[2,64,2048]{2,1,0:T(8,128)(2,1)} %get-tuple-element.157), channel_id=1, source_target_pairs={{0,2},{1,3},{2,0},{3,1},{4,6},{5,7},{6,4},{7,5},{8,10},{9,11},{10,... | collective-permute-start | bytes 1572872 | tf_op jit(solution)/shard_map/ppermute | solution.py:660
  275.9 22.3 %collective-permute-start.36 = (bf16[2,64,2048]{2,1,0:T(8,128)(2,1)}, bf16[2,64,2048]{2,1,0:T(8,128)(2,1)}, u32[]{:S(2)}, u32[]{:S(2)}) collective-permute-start(bf16[2,64,2048]{2,1,0:T(8,128)(2,1)} %get-tuple-element.157), channel_id=1, source_target_pairs={{0,3},{1,2},{2,1},{3,0},{4,7},{5,6},{6,5},{7,4},{8,11},{9,10},{10,... | collective-permute-start | bytes 1572872 | tf_op jit(solution)/shard_map/ppermute | solution.py:660
  290.1 73.9 %all-to-all-start.4 = ((bf16[8,256,640]{2,1,0:T(8,128)(2,1)}), bf16[8,256,640]{2,1,0:T(8,128)(2,1)S(1)}, u32[]{:S(2)}, u32[]{:S(2)}) async-start(bf16[8,256,640]{2,1,0:T(8,128)(2,1)} %bitcast.224), calls=%async_computation.4 | async-start | bytes 5242880 | tf_op jit(solution)/shard_map/all_to_all | solution.py:592
  298.2 26.1 %collective-permute-start.38 = (bf16[2,64,2048]{2,1,0:T(8,128)(2,1)S(1)}, bf16[2,64,2048]{2,1,0:T(8,128)(2,1)S(1)}, u32[]{:S(2)}, u32[]{:S(2)}) collective-permute-start(bf16[2,64,2048]{2,1,0:T(8,128)(2,1)S(1)} %convert_add_fusion.6), channel_id=1, source_target_pairs={{0,3},{1,2},{2,1},{3,0},{4,7},{5,6},{6,5},{7,4},{8,11},{9,10},{10,... | collective-permute-start | bytes 1572872 | tf_op jit(solution)/shard_map/ppermute | solution.py:660
  301.0 23.7 %collective-permute-start.40 = (bf16[2,64,2048]{2,1,0:T(8,128)(2,1)S(1)}, bf16[2,64,2048]{2,1,0:T(8,128)(2,1)S(1)}, u32[]{:S(2)}, u32[]{:S(2)}) collective-permute-start(bf16[2,64,2048]{2,1,0:T(8,128)(2,1)S(1)} %convert_add_fusion.5), channel_id=1, source_target_pairs={{0,2},{1,3},{2,0},{3,1},{4,6},{5,7},{6,4},{7,5},{8,10},{9,11},{10,... | collective-permute-start | bytes 1572872 | tf_op jit(solution)/shard_map/ppermute | solution.py:660
  302.4 22.3 %collective-permute-start.42 = (bf16[2,64,2048]{2,1,0:T(8,128)(2,1)S(1)}, bf16[2,64,2048]{2,1,0:T(8,128)(2,1)S(1)}, u32[]{:S(2)}, u32[]{:S(2)}) collective-permute-start(bf16[2,64,2048]{2,1,0:T(8,128)(2,1)S(1)} %convert_add_fusion.4), channel_id=1, source_target_pairs={{0,1},{1,0},{2,3},{3,2},{4,5},{5,4},{6,7},{7,6},{8,9},{9,8},{10,11... | collective-permute-start | bytes 1572872 | tf_op jit(solution)/shard_map/ppermute | solution.py:660
  338.1 24.5 %collective-permute-start.55 = (bf16[2,64,2048]{2,1,0:T(8,128)(2,1)S(1)}, bf16[2,64,2048]{2,1,0:T(8,128)(2,1)S(1)}, u32[]{:S(2)}, u32[]{:S(2)}) collective-permute-start(bf16[2,64,2048]{2,1,0:T(8,128)(2,1)S(1)} %add_convert_fusion.1), channel_id=1, source_target_pairs={{0,2},{1,3},{2,0},{3,1},{4,6},{5,7},{6,4},{7,5},{8,10},{9,11},{10,... | collective-permute-start | bytes 1572872 | tf_op jit(solution)/shard_map/ppermute | solution.py:660
  339.2 23.4 %collective-permute-start.57 = (bf16[2,64,2048]{2,1,0:T(8,128)(2,1)S(1)}, bf16[2,64,2048]{2,1,0:T(8,128)(2,1)S(1)}, u32[]{:S(2)}, u32[]{:S(2)}) collective-permute-start(bf16[2,64,2048]{2,1,0:T(8,128)(2,1)S(1)} %add_convert_fusion), channel_id=1, source_target_pairs={{0,1},{1,0},{2,3},{3,2},{4,5},{5,4},{6,7},{7,6},{8,9},{9,8},{10,11... | collective-permute-start | bytes 1572872 | tf_op jit(solution)/shard_map/ppermute | solution.py:660
  364.0 58.0 %all-to-all-start.5 = ((bf16[8,264,384]{2,1,0:T(8,128)(2,1)}), bf16[8,264,384]{2,1,0:T(8,128)(2,1)}, u32[]{:S(2)}, u32[]{:S(2)}) async-start(bf16[8,264,384]{2,1,0:T(8,128)(2,1)} %fusion.1), calls=%async_computation.5 | async-start | bytes 3244032 | tf_op jit(solution)/shard_map/all_to_all | solution.py:592
  369.8 31.4 %collective-permute-start.58 = (bf16[64,2048]{1,0:T(8,128)(2,1)S(1)}, bf16[64,2048]{1,0:T(8,128)(2,1)S(1)}, u32[]{:S(2)}, u32[]{:S(2)}) collective-permute-start(bf16[64,2048]{1,0:T(8,128)(2,1)S(1)} %fusion.16), channel_id=1, source_target_pairs={{0,8},{8,0},{1,9},{9,1},{2,10},{10,2},{3,11},{11,3},{4,12},{12,4},... | collective-permute-start | bytes 786440 | tf_op jit(solution)/shard_map/ppermute | solution.py:596
  423.3 22.7 %collective-permute-start.49 = (bf16[64,2048]{1,0:T(8,128)(2,1)S(1)}, bf16[64,2048]{1,0:T(8,128)(2,1)}, u32[]{:S(2)}, u32[]{:S(2)}) collective-permute-start(bf16[64,2048]{1,0:T(8,128)(2,1)S(1)} %fusion.15), channel_id=1, source_target_pairs={{0,8},{8,0},{1,9},{9,1},{2,10},{10,2},{3,11},{11,3},{4,12},{12,4},... | collective-permute-start | bytes 786440 | tf_op jit(solution)/shard_map/ppermute | solution.py:596
  (95 other events, 986.0 us)
